TPU v7x, 128 devices: a whole 4x4x4 slice. The times are simulated.
128 devices in a mesh: row: 16 (over z, y), col: 8 (over x, core).
Axes of the slice: x: 4, y: 4, z: 4, core: 2. Of those that a mesh axis runs over, the one named last changes fastest.
Arguments:
- frames: bfloat16 [16384, 4096], P('row', 'col'), may hold values from -6 to 6
- w_value: bfloat16 [4096, 4096], P('row', 'col'), may hold values from -0.09375 to 0.09375
- w_gate: bfloat16 [4096, 4096], P('row', 'col'), may hold values from -0.09375 to 0.09375
- taps: bfloat16 [31, 4096], P(None, 'col'), may hold values from -1 to 1
- grad_out: bfloat16 [16384, 4096], P('row', 'col'), may hold values from -4 to 4
Outputs:
- activated: bfloat16 [16384, 4096], P('row', 'col')
- grad_frames: bfloat16 [16384, 4096], P('row', 'col')
- grad_value: bfloat16 [4096, 4096], P('row', 'col')
- grad_gate: bfloat16 [4096, 4096], P('row', 'col')
- grad_taps: float32 [31, 4096], P(None, 'col')
All inputs are finite; a program needn't handle non-finite values.
Results may differ from a plain program's by a relative error of at most 0.019.
Values may be sent and summed in bfloat16 or wider, within the bound.
No kernel may reach another device: no remote copies, remote signals or barrier semaphores. Data moves between devices by JAX's collectives and lax.ppermute only.
A program may use at most 128 MiB of HBM per device.

v0:
```python
import jax
import jax.numpy as jnp
from jax import lax
from jax.sharding import PartitionSpec as P


def padded(array, sides, width):
    for axis, dim in sides:
        count, length = (lax.axis_size(axis), array.shape[dim])
        up = [(i, (i + 1) % count) for i in range(count - 1)]
        down = [(j, i) for i, j in up]
        last = lax.slice_in_dim(array, length - width, length, axis=dim)
        initial = lax.slice_in_dim(array, 0, width, axis=dim)
        before = lax.ppermute(last, axis, up)
        after = lax.ppermute(initial, axis, down)
        array = jnp.concatenate([before, array, after], axis=dim)
    return array


def widen(field, half):
    return padded(field, (("row", 0),), half)


def per_device(frames, w_value, w_gate, taps, grad_out):
    width = taps.shape[0]
    half = (width - 1) // 2
    kernel = taps.astype(jnp.float32)
    local_rows = frames.shape[0]
    channels = w_value.shape[1]
    contract = (((1,), (1,)), ((), ()))
    whole = lax.all_gather(frames, "col", axis=1, tiled=True)
    full_value, full_gate = (
        lax.all_gather(w_value, "row", axis=0, tiled=True),
        lax.all_gather(w_gate, "row", axis=0, tiled=True),
    )
    value = jnp.dot(whole, full_value, preferred_element_type=jnp.float32)
    gate = jnp.dot(whole, full_gate, preferred_element_type=jnp.float32)
    gate_prob = jax.nn.sigmoid(gate)
    glu = (value * gate_prob).astype(jnp.bfloat16)
    glu_pad = widen(glu, half)
    filtered = jnp.zeros((local_rows, channels), jnp.float32)
    for k in range(width):
        filtered = filtered + kernel[k] * glu_pad[k : k + local_rows].astype(jnp.float32)
    prob = jax.nn.sigmoid(filtered)
    activated = (filtered * prob).astype(jnp.bfloat16)
    grad_filtered = (grad_out.astype(jnp.float32) * (prob + filtered * prob * (1.0 - prob))).astype(
        jnp.bfloat16
    )
    grad_pad = widen(grad_filtered, half)
    grad_glu = jnp.zeros((local_rows, channels), jnp.float32)
    for k in range(width):
        grad_glu = grad_glu + kernel[k] * grad_pad[2 * half - k : 2 * half - k + local_rows].astype(
            jnp.float32
        )
    grad_float = grad_filtered.astype(jnp.float32)
    tap_part = jnp.stack(
        [
            jnp.sum(grad_float * glu_pad[k : k + local_rows].astype(jnp.float32), axis=0)
            for k in range(width)
        ]
    )
    grad_taps = lax.psum(tap_part.astype(jnp.bfloat16), "row").astype(jnp.float32)
    grad_val = (grad_glu * gate_prob).astype(jnp.bfloat16)
    grad_gt = (grad_glu * value * gate_prob * (1.0 - gate_prob)).astype(jnp.bfloat16)
    partial_sum = lax.dot_general(
        grad_val, full_value, contract, preferred_element_type=jnp.float32
    )
    partial_sum = partial_sum + lax.dot_general(
        grad_gt, full_gate, contract, preferred_element_type=jnp.float32
    )
    grad_frames = lax.psum_scatter(
        partial_sum.astype(jnp.bfloat16), "col", scatter_dimension=1, tiled=True
    )
    both = jnp.concatenate([grad_val, grad_gt], axis=1)
    summed = lax.psum_scatter(
        lax.dot_general(
            whole, both, (((0,), (0,)), ((), ())), preferred_element_type=jnp.float32
        ).astype(jnp.bfloat16),
        "row",
        scatter_dimension=0,
        tiled=True,
    ).astype(jnp.float32)
    grad_value = summed[:, :channels].astype(jnp.bfloat16)
    grad_gate = summed[:, channels:].astype(jnp.bfloat16)
    return (activated, grad_frames, grad_value, grad_gate, grad_taps)


def solution(mesh):
    in_specs = (P("row", "col"), P("row", "col"), P("row", "col"), P(None, "col"), P("row", "col"))
    out_specs = (P("row", "col"), P("row", "col"), P("row", "col"), P("row", "col"), P(None, "col"))
    return jax.shard_map(
        per_device, mesh=mesh, in_specs=in_specs, out_specs=out_specs, check_vma=False
    )
```

profile of v0, /device:TPU:42, one launch (start us, length us, event | category | flops | bytes accessed | tf_op | source)
XLA Modules:
  0.0 391.2 jit_solution(13274862951386971952)
XLA Ops:
  7.2 0.0 all-gather.8.cloned.1.call-start
  7.2 0.7 all-gather.8.cloned.1.call-update
  7.9 0.0 all-gather.4.cloned.1.call-start
  7.9 0.7 all-gather.4.cloned.1.call-update
  8.6 0.0 all-gather.6.cloned.1.call-start
  8.7 0.7 all-gather.6.cloned.1.call-update
  9.4 0.0 reduce-scatter.5.cloned.1.call-start
  9.4 1.0 fusion.144
  10.5 51.9 %all-gather.8.cloned.1.call-done = bf16[4096,512]{1,0:T(8,128)(2,1)} async-done(((bf16[256,512]{1,0:T(8,128)(2,1)}), bf16[4096,512]{1,0:T(8,128)(2,1)}) %all-gather.8.cloned.1.call-update) | async-done | bytes 4194320 | tf_op jit(solution)/shard_map/all_gather | solution.py:34
  62.3 51.6 %all-gather.4.cloned.1.call-done = bf16[1024,4096]{1,0:T(8,128)(2,1)} async-done(((bf16[1024,512]{1,0:T(8,128)(2,1)}), bf16[1024,4096]{1,0:T(8,128)(2,1)}) %all-gather.4.cloned.1.call-update) | async-done | bytes 8388624 | tf_op jit(solution)/shard_map/all_gather | solution.py:31
  113.9 10.7 %add_divide_fusion.1 = f32[1024,512]{1,0:T(8,128)} fusion(bf16[1024,4096]{1,0:T(8,128)(2,1)} %all-gather.4.cloned.1.call-done, bf16[4096,512]{1,0:T(8,128)(2,1)} %all-gather.8.cloned.1.call-done), kind=kOutput, calls=%fused_computation.206 | convolution fusion | flops 4296540160 | bytes 14680064 | tf_op jit(solution)/shard_map/dot_general | solution.py:37
  124.6 0.0 copy-start.2
  124.7 0.0 copy-start.1
  124.7 42.7 %all-gather.6.cloned.1.call-done = bf16[4096,512]{1,0:T(8,128)(2,1)} async-done(((bf16[256,512]{1,0:T(8,128)(2,1)}), bf16[4096,512]{1,0:T(8,128)(2,1)}) %all-gather.6.cloned.1.call-update) | async-done | bytes 4194320 | tf_op jit(solution)/shard_map/all_gather | solution.py:33
  167.4 9.7 %multiply_convert_fusion.3 = (bf16[1024,512]{1,0:T(8,128)(2,1)S(1)}, f32[1024,512]{1,0:T(8,128)S(1)}) fusion(f32[1024,512]{1,0:T(8,128)} %add_divide_fusion.1, bf16[1024,4096]{1,0:T(8,128)(2,1)} %all-gather.4.cloned.1.call-done, bf16[4096,512]{1,0:T(8,128)(2,1)} %all-gather.6.cloned.1.call-done), kind=kOutput, calls=%fused_computation.205 | convolution fusion | flops 4296015872 | bytes 17825792 | tf_op jit(solution)/shard_map/dot_general | solution.py:36
  177.1 3.4 collective-permute-start
  180.5 2.5 collective-permute-start.1
  183.0 0.0 copy-done.2
  183.0 0.0 collective-permute-done
  183.0 3.1 collective-permute-done.1
  186.2 0.0 copy-done.1
  186.2 0.0 copy-start
  186.2 0.0 slice-start
  186.2 17.7 %fusion.75 = (bf16[512]{0:T(512)(128)(2,1)S(1)}, bf16[512]{0:T(512)(128)(2,1)S(1)}, bf16[512]{0:T(512)(128)(2,1)S(1)}, bf16[512]{0:T(512)(128)(2,1)S(1)}, bf16[5...) fusion(bf16[15,512]{1,0:T(8,128)(2,1)S(1)} %collective-permute-done.1,, ...), kind=kLoop, calls=%fused_computation.196 | loop fusion | flops 120058880 | bytes 5343232 | tf_op jit(solution)/shard_map/reduce_sum | solution.py:58
  203.9 4.0 %collective-permute-start.2 = (bf16[15,512]{1,0:T(8,128)(2,1)S(1)}, bf16[15,512]{1,0:T(8,128)(2,1)S(1)}, u32[]{:S(2)}, u32[]{:S(2)}) collective-permute-start(bf16[15,512]{1,0:T(8,128)(2,1)S(1)} %get-tuple-element.48), channel_id=1, source_target_pairs={{8,0},{16,8},{24,16},{32,24},{40,32},{48,40},{56,48},{64,56},{72,6... | collective-permute-start | bytes 46088 | tf_op jit(solution)/shard_map/ppermute | solution.py:15
  207.9 2.1 collective-permute-start.3
  210.0 0.0 collective-permute-done.2
  210.0 5.9 %collective-permute-done.3 = bf16[15,512]{1,0:T(8,128)(2,1)S(1)} collective-permute-done((bf16[15,512]{1,0:T(8,128)(2,1)S(1)}, bf16[15,512]{1,0:T(8,128)(2,1)S(1)}, u32[]{:S(2)}, u32[]{:S(2)}) %collective-permute-start.3) | collective-permute-done | bytes 15392 | tf_op jit(solution)/shard_map/ppermute | solution.py:14
  215.9 0.0 copy-done
  215.9 0.0 slice-start.1
  215.9 14.7 %multiply_convert_fusion = (bf16[1024,512]{1,0:T(8,128)(2,1)S(1)}, f32[1024,512]{1,0:T(8,128)S(1)}) fusion(f32[1024,512]{1,0:T(8,128)S(1)} %copy-done, f32[1024,512]{1,0:T(8,128)S(1)} %get-tuple-element.86, bf16[1024,512]{1,0:T(8,128)(2,1)S(1)} %get-tuple-element.44, bf16[15,512]{1,0:T(8,128)(2,1)S(1)} %collective-permute-done.3, f32[512]{0:T(512)S(1)} %bitcast.103, ...), kind=kLoop, calls=%fused_computation.201 | loop fusion | flops 98041856 | bytes 8482816 | tf_op jit(solution)/shard_map/convert_element_type | solution.py:64
  230.6 1.3 multiply_convert_fusion.1
  232.0 0.0 slice-done
  232.0 0.0 slice-done.1
  232.0 12.5 %convert_bitcast_fusion = bf16[4096,1024]{0,1:T(8,128)(2,1)} fusion(bf16[1024,4096]{1,0:T(8,128)(2,1)S(1)} %bitcast.105, bf16[1024,512]{1,0:T(8,128)(2,1)S(1)} %get-tuple-element.46, bf16[1024,512]{1,0:T(8,128)(2,1)} %multiply_convert_fusion.1), kind=kOutput, calls=%fused_computation.33 | convolution fusion | flops 8598323200 | bytes 18874368 | tf_op jit(solution)/shard_map/dot_general | solution.py:76
  244.5 0.0 reduce-scatter.5.cloned.1.call-update
  244.5 0.3 reduce-scatter.3.cloned.1.call-start
  244.8 13.0 %fusion.146 = f32[1024,4096]{1,0:T(8,128)} fusion(bf16[1024,512]{1,0:T(8,128)(2,1)} %multiply_convert_fusion.1, bf16[4096,512]{1,0:T(8,128)(2,1)} %all-gather.6.cloned.1.call-done), kind=kOutput, calls=%fused_computation.291 | convolution fusion | flops 4294967296 | bytes 22020096 | tf_op jit(solution)/shard_map/dot_general | solution.py:65
  257.8 11.5 %add_convert_fusion = bf16[1024,4096]{1,0:T(8,128)(2,1)} fusion(f32[1024,4096]{1,0:T(8,128)} %fusion.146, bf16[1024,512]{1,0:T(8,128)(2,1)S(1)} %get-tuple-element.46, bf16[4096,512]{1,0:T(8,128)(2,1)} %all-gather.8.cloned.1.call-done), kind=kOutput, calls=%fused_computation.32 | convolution fusion | flops 4303355904 | bytes 30408704 | tf_op jit(solution)/shard_map/dot_general | solution.py:68
  269.3 0.0 reduce-scatter.3.cloned.1.call-update
  269.4 2.0 fusion.60
  271.5 2.1 fusion.74
  273.6 2.0 fusion.59
  275.7 2.5 fusion.76
  278.4 0.2 stack.159
  278.5 62.4 %psum.7 = bf16[31,512]{1,0:T(8,128)(2,1)S(1)} all-reduce(bf16[31,512]{1,0:T(8,128)(2,1)S(1)} %stack.159), channel_id=1, replica_groups=mesh['row'=16,'col'=8] {'row'}, use_global_device_ids=true, to_apply=%region_33.0 | all-reduce | flops 15872 | bytes 63488 | tf_op jit(solution)/shard_map/psum | solution.py:62
  341.0 0.6 convert_element_type.327
  341.6 3.1 fusion.81
  344.7 0.0 reduce-scatter.5.cloned.1.call-done
  344.7 1.1 fusion.143
  345.8 0.8 copy.11
  346.7 0.8 copy.10
  347.5 37.2 %reduce-scatter.3.cloned.1.call-done = bf16[1024,512]{1,0:T(8,128)(2,1)} async-done(((bf16[1024,4096]{1,0:T(8,128)(2,1)}), bf16[1024,512]{1,0:T(8,128)(2,1)}) %reduce-scatter.3.cloned.1.call-update) | async-done | bytes 1048592 | tf_op jit(solution)/shard_map/reduce_scatter | solution.py:71
  (35 shorter events, 0.2 us)
Async XLA Ops:
  7.2 55.2 %all-gather.8.cloned.1.call-start = ((), (), s32[]{:S(2)}) async-start(), calls=%async_computation.4 | async-start | bytes 4456448 | tf_op jit(solution)/shard_map/all_gather | solution.py:34
  7.9 106.0 %all-gather.4.cloned.1.call-start = ((), (), s32[]{:S(2)}) async-start(), calls=%async_computation.2 | async-start | bytes 9437184 | tf_op jit(solution)/shard_map/all_gather | solution.py:31
  8.6 158.7 %all-gather.6.cloned.1.call-start = ((), (), s32[]{:S(2)}) async-start(), calls=%async_computation.3 | async-start | bytes 4456448 | tf_op jit(solution)/shard_map/all_gather | solution.py:33
  9.4 335.4 %reduce-scatter.5.cloned.1.call-start = ((), (), s32[]{:S(2)}) async-start(), calls=%async_computation.6 | async-start | bytes 8912896 | tf_op jit(solution)/shard_map/reduce_scatter | solution.py:75
  124.6 58.3 %copy-start.2 = (bf16[31,512]{1,0:T(8,128)(2,1)S(1)}, bf16[31,512]{1,0:T(8,128)(2,1)}, u32[]{:S(2)}) copy-start(bf16[31,512]{1,0:T(8,128)(2,1)} %param.8) | copy-start | bytes 95236
  124.7 61.5 %copy-start.1 = (bf16[1024,512]{1,0:T(8,128)(2,1)S(1)}, bf16[1024,512]{1,0:T(8,128)(2,1)}, u32[]{:S(2)}) copy-start(bf16[1024,512]{1,0:T(8,128)(2,1)} %param.9) | copy-start | bytes 3145732
  177.1 5.9 %collective-permute-start = (bf16[15,512]{1,0:T(8,128)(2,1)S(1)}, bf16[15,512]{1,0:T(8,128)(2,1)S(1)}, u32[]{:S(2)}, u32[]{:S(2)}) collective-permute-start(bf16[15,512]{1,0:T(8,128)(2,1)S(1)} %get-tuple-element.50), channel_id=1, source_target_pairs={{0,8},{8,16},{16,24},{24,32},{32,40},{40,48},{48,56},{56,64},{64,7... | collective-permute-start | bytes 46088 | tf_op jit(solution)/shard_map/ppermute | solution.py:14
  180.5 5.6 %collective-permute-start.1 = (bf16[15,512]{1,0:T(8,128)(2,1)S(1)}, bf16[15,512]{1,0:T(8,128)(2,1)S(1)}, u32[]{:S(2)}, u32[]{:S(2)}) collective-permute-start(bf16[15,512]{1,0:T(8,128)(2,1)S(1)} %get-tuple-element.51), channel_id=1, source_target_pairs={{8,0},{16,8},{24,16},{32,24},{40,32},{48,40},{56,48},{64,56},{72,6... | collective-permute-start | bytes 46088 | tf_op jit(solution)/shard_map/ppermute | solution.py:15
  186.2 29.7 %copy-start = (f32[1024,512]{1,0:T(8,128)S(1)}, f32[1024,512]{1,0:T(8,128)}, u32[]{:S(2)}) copy-start(f32[1024,512]{1,0:T(8,128)} %add_divide_fusion.1) | copy-start | bytes 6291460
  186.2 45.8 %slice-start = ((s8[8388608]{0:T(1024)(128)(4,1)}), s8[4194304]{0:T(1024)(128)(4,1)S(1)}, s32[]{:S(2)}) async-start(s8[8388608]{0:T(1024)(128)(4,1)} %bitcast.104), calls=%async_computation.7 | async-start | bytes 8388608
  203.9 6.1 %collective-permute-start.2 = (bf16[15,512]{1,0:T(8,128)(2,1)S(1)}, bf16[15,512]{1,0:T(8,128)(2,1)S(1)}, u32[]{:S(2)}, u32[]{:S(2)}) collective-permute-start(bf16[15,512]{1,0:T(8,128)(2,1)S(1)} %get-tuple-element.48), channel_id=1, source_target_pairs={{8,0},{16,8},{24,16},{32,24},{40,32},{48,40},{56,48},{64,56},{72,6... | collective-permute-start | bytes 46088 | tf_op jit(solution)/shard_map/ppermute | solution.py:15
  207.9 8.0 %collective-permute-start.3 = (bf16[15,512]{1,0:T(8,128)(2,1)S(1)}, bf16[15,512]{1,0:T(8,128)(2,1)S(1)}, u32[]{:S(2)}, u32[]{:S(2)}) collective-permute-start(bf16[15,512]{1,0:T(8,128)(2,1)S(1)} %get-tuple-element.49), channel_id=1, source_target_pairs={{0,8},{8,16},{16,24},{24,32},{32,40},{40,48},{48,56},{56,64},{64,7... | collective-permute-start | bytes 46088 | tf_op jit(solution)/shard_map/ppermute | solution.py:14
  215.9 16.0 %slice-start.1 = ((s8[8388608]{0:T(1024)(128)(4,1)}), s8[4194304]{0:T(1024)(128)(4,1)S(1)}, s32[]{:S(2)}) async-start(s8[8388608]{0:T(1024)(128)(4,1)} %bitcast.104), calls=%async_computation.8 | async-start | bytes 8388608
  244.5 140.2 %reduce-scatter.3.cloned.1.call-start = ((), (), s32[]{:S(2)}) async-start(), calls=%async_computation.5 | async-start | bytes 9437184 | tf_op jit(solution)/shard_map/reduce_scatter | solution.py:71
Sparse Core Ops, SparseCore 0:
  10.1 52.1 all-gather.7
  64.0 49.8 all-gather.3
  116.1 51.2 all-gather.5
  244.6 86.1 reduce-scatter.4
  333.6 51.0 reduce-scatter.2
where the time goes:
time: 394 us; the launch traced here: 391 us
  waiting for transfers between devices  194 us (49%)
  blocking collectives  62.4 us (16%)
  matrix products  57.5 us (15%)
  other arithmetic  46.2 us (12%)
  between operations  14.1 us (4%)
  starting transfers between devices  12.3 us (3%)
  local copies, waits for them, and re-layouts  4.16 us (1%)
    psum x1, blocking collectives, per_device(): lax.psum(tap_part.astype(jnp.bfloat16), 'row').astype(jnp.float32)  62.4 us
    all_gather x1, waiting for transfers between devices, per_device(): lax.all_gather(w_gate, 'row', axis=0, tiled=True)  51.9 us
    all_gather x1, waiting for transfers between devices, per_device(): whole = lax.all_gather(frames, 'col', axis=1, tiled=True)  51.6 us
    all_gather x1, waiting for transfers between devices, per_device(): lax.all_gather(w_value, 'row', axis=0, tiled=True)  42.7 us
    reduce_scatter x1, waiting for transfers between devices, per_device(): lax.psum_scatter(partial_sum.astype(jnp.bfloat16), 'col', scatter_dimensi...  37.2 us
    reduce_sum x5, other arithmetic, per_device(): jnp.sum(grad_float * glu_pad[k:k + local_rows].astype(jnp.float32), axis=0)  26.4 us
    convert_element_type x1, other arithmetic, per_device(): (grad_glu * value * gate_prob * (1.0 - gate_prob)).astype(jnp.bfloat16)  14.7 us
    dot_general x1, matrix products, per_device(): lax.dot_general(grad_val, full_value, contract, preferred_element_type=jn...  13 us
  transfers between devices with their start and end apart: 9, of which 6 were waited for; matrix products, arithmetic and copies ran while one was open for 13% of the time, Pallas kernels for 0%

commit v1 on v0

v1 whole, which is shorter than its diff:
```python
import functools

import jax
import jax.numpy as jnp
from jax import lax
from jax.experimental import pallas as pl
from jax.experimental.pallas import tpu as pltpu
from jax.sharding import PartitionSpec as P

F32 = jnp.float32
BF16 = jnp.bfloat16
BOTH = ("row", "col")
RING = 4
CORES = 2
EDGE = 32
LANES = 128
STRIP = 32
MIB = 2**20


def turning(step):
    pairs = []
    for source in range(RING * RING * RING * CORES):
        rest, core = source // CORES, source % CORES
        at = [rest // RING**2, rest // RING % RING, rest % RING]
        at, core = step(at, core)
        z, y, x = (place % RING for place in at)
        pairs.append((source, ((z * RING + y) * RING + x) * CORES + core))
    return pairs


def way(core):
    return 1 - 2 * core


ALONG_Y = turning(lambda at, core: ((at[0], at[1] + way(core), at[2]), core))
ALONG_Z = turning(lambda at, core: ((at[0] + way(core), at[1], at[2]), core))
BACK_Y = turning(lambda at, core: ((at[0], at[1] - way(core), at[2]), core))
BACK_Z = turning(lambda at, core: ((at[0] - way(core), at[1], at[2]), core))
TWO_Y = turning(lambda at, core: ((at[0], at[1] + 2, at[2]), core))
TWO_Z = turning(lambda at, core: ((at[0] + 2, at[1], at[2]), core))
UP_Y = turning(lambda at, core: ((at[0], at[1] + 1, at[2]), core))
UP_Z = turning(lambda at, core: ((at[0] + 1, at[1], at[2]), core))
DOWN_Y = turning(lambda at, core: ((at[0], at[1] - 1, at[2]), core))
DOWN_Z = turning(lambda at, core: ((at[0] - 1, at[1], at[2]), core))
OFFSETS = (0, -1, 1, 2)


def send(array, pairs):
    return lax.ppermute(array, BOTH, pairs)


def halo(array):
    count, length = lax.axis_size("row"), array.shape[0]
    up = [(i, i + 1) for i in range(count - 1)]
    down = [(j, i) for i, j in up]
    before = lax.ppermute(array[length - EDGE :], "row", up)
    after = lax.ppermute(array[:EDGE], "row", down)
    return before, after


def together(*values):
    return lax.optimization_barrier(values)


def middle_body(width, rows, place, *refs):
    pieces, (before, inner, after), (gout, taps) = refs[:10], refs[10:13], refs[13:15]
    act, turned_both, frames_out, first_out, gtap = refs[15:20]
    vg, glu, gf, gate_s, vg_s, both, whole, weights, in_sem = refs[20:]
    half = (width - 1) // 2
    total = whole.shape[0]
    depth, channels = weights.shape[1], weights.shape[2] // 2
    strip = pl.program_id(0)
    strips = channels // LANES
    z, y, turn = place[0], place[1], place[2]
    copies = [
        (before, whole.at[pl.ds(0, EDGE), :]),
        (inner, whole.at[pl.ds(EDGE, rows), :]),
        (after, whole.at[pl.ds(EDGE + rows, EDGE), :]),
    ]
    for kind in range(2):
        for far in range(RING):
            for near in range(RING):
                if far < RING - 1:
                    source = pieces[5 * kind + far].at[near]
                else:
                    source = pieces[5 * kind + far + near // 2].at[near % 2]
                a, b = (near, far) if kind else (far, near)
                row = lax.rem(z + OFFSETS[a] + RING, RING) * RING
                row = row + lax.rem(y + OFFSETS[b] + RING, RING)
                copies.append((source, weights.at[row, :, pl.ds(kind * channels, channels)]))
    copies = [
        pltpu.make_async_copy(source, target, in_sem.at[n])
        for n, (source, target) in enumerate(copies)
    ]
    @pl.when(strip == 0)
    def _():
        for copy in copies:
            copy.start()
        for copy in copies:
            copy.wait()

    @pl.when(strip < strips)
    def _():
        def columns(kind):
            start = pl.multiple_of(kind * channels + strip * LANES, LANES)
            return weights[:, :, pl.ds(start, LANES)].reshape(RING * RING * depth, LANES)

        vg[...] = jnp.dot(
            whole[...], jnp.concatenate([columns(0), columns(1)], axis=1), preferred_element_type=F32
        )

        def gates(i, _):
            at = pl.ds(pl.multiple_of(i * STRIP, STRIP), STRIP)
            p = jax.nn.sigmoid(vg[at, LANES:])
            vp = vg[at, :LANES] * p
            glu[at, :] = vp.astype(BF16).astype(F32)
            gate_s[at, :] = p
            vg_s[at, :] = vp * (1.0 - p)
            return 0

        lax.fori_loop(0, total // STRIP, gates, 0)
        tap = [jnp.broadcast_to(taps[k : k + 1, :], (8, LANES)) for k in range(width)]

        def conv(source, start, sign):
            parts = [jnp.zeros((8, LANES), F32) for _ in range(STRIP // 8)]
            for k in range(width):
                x = source[pl.ds(start + sign * (k - half), STRIP), :]
                for j in range(STRIP // 8):
                    parts[j] = parts[j] + tap[k] * x[8 * j : 8 * j + 8]
            return jnp.concatenate(parts, axis=0)

        gf[0:EDGE, :] = jnp.zeros((EDGE, LANES), F32)
        gf[total - EDGE : total, :] = jnp.zeros((EDGE, LANES), F32)

        def forward(i, _):
            start = pl.multiple_of(i * STRIP, 16) + EDGE // 2
            at = pl.ds(start, STRIP)
            f = conv(glu, start, 1)
            s = jax.nn.sigmoid(f)
            fs = f * s
            vg[at, :LANES] = fs
            g = gout[at, :].astype(F32) * (s + fs * (1.0 - s))
            gf[at, :] = g.astype(BF16).astype(F32)
            return 0

        lax.fori_loop(0, (rows + EDGE) // STRIP, forward, 0)
        act[...] = vg[EDGE : EDGE + rows, :LANES].astype(BF16)

        def backward(i, _):
            start = pl.multiple_of(i * STRIP, STRIP) + EDGE
            at = pl.ds(start, STRIP)
            d = conv(gf, start, -1)
            vg[at, :LANES] = d * gate_s[at, :]
            vg[at, LANES:] = d * vg_s[at, :]
            return 0

        lax.fori_loop(0, rows // STRIP, backward, 0)
        for kind in range(2):
            grad = vg[EDGE : EDGE + rows, kind * LANES : (kind + 1) * LANES]
            start = pl.multiple_of(kind * channels + strip * LANES, LANES)
            both[:, pl.ds(start, LANES)] = grad.astype(BF16)
            turned_both[kind, pl.ds(pl.multiple_of(strip * LANES, LANES), LANES), :] = grad.T.astype(
                BF16
            )

        def tap_sums(i, total_sums):
            start = pl.multiple_of(i * STRIP, STRIP) + EDGE
            q = gf[pl.ds(start, STRIP), :]
            out = []
            for k in range(width):
                x = glu[pl.ds(start + k - half, STRIP), :] * q
                t = total_sums[k]
                for j in range(STRIP // 8):
                    t = t + x[8 * j : 8 * j + 8]
                out.append(t)
            return tuple(out)

        start_sums = tuple(jnp.zeros((8, LANES), F32) for _ in range(width))
        sums = lax.fori_loop(0, rows // STRIP, tap_sums, start_sums)
        for k in range(width):
            gtap[k : k + 1, :] = jnp.sum(sums[k], axis=0, keepdims=True)
        gtap[width:, :] = jnp.zeros((gtap.shape[0] - width, LANES), F32)

    @pl.when((strip >= strips) & (strip < strips + RING * CORES))
    def _():
        block = weights[pl.ds((strip - strips) * CORES, CORES)].reshape(-1, 2 * channels)
        frames_out[...] = lax.dot_general(
            both[...], block, (((1,), (1,)), ((), ())), preferred_element_type=F32
        ).astype(BF16)

    for kind in range(2):

        @pl.when(strip == strips + RING * CORES + kind)
        def _():
            for q in range(RING):
                far = lax.rem(y + RING - turn, RING) if kind else lax.rem(z + RING - turn, RING)
                near = (z if kind else y) + 2 * RING - (q + 1) * turn
                near = lax.rem(near, RING)
                row = near * RING + far if kind else far * RING + near
                part = whole[EDGE : EDGE + rows, pl.ds(pl.multiple_of(row * depth, LANES), depth)]
                first_out[0, q] = jnp.dot(
                    turned_both[kind], part, preferred_element_type=F32
                ).astype(BF16)


def middle(place, pieces, parts, gout, taps):
    rows, inner = parts[1].shape
    total = rows + 2 * EDGE
    depth, channels = pieces[0].shape[1:]
    width = taps.shape[0]
    tall = -(-width // 8) * 8
    taps = jnp.pad(taps.astype(F32), ((0, tall - width), (0, 0)))

    def strips(n):
        return pl.BlockSpec((n, LANES), lambda j, place: (0, jnp.minimum(j, count - 1)))

    def far():
        return pl.BlockSpec(memory_space=pltpu.HBM)

    count = channels // LANES
    part = inner // (RING * CORES)
    begin, end = count, count + RING * CORES

    def frames_block(j, place):
        return (0, jnp.clip(j - begin, 0, RING * CORES - 1))

    def first_block(j, place):
        return (jnp.maximum(j - end, 0), 0, 0, 0)

    shape = jax.ShapeDtypeStruct
    return pl.pallas_call(
        functools.partial(middle_body, width, rows),
        grid_spec=pltpu.PrefetchScalarGridSpec(
            num_scalar_prefetch=1,
            grid=(end + 2,),
            in_specs=[far() for _ in range(len(pieces) + len(parts))] + [strips(total), strips(tall)],
            out_specs=[
                strips(rows),
                pl.BlockSpec((2, channels, rows), lambda j, place: (0, 0, 0)),
                pl.BlockSpec((rows, part), frames_block),
                pl.BlockSpec((1, RING, channels, depth), first_block),
                strips(tall),
            ],
            scratch_shapes=[pltpu.VMEM((total, 2 * LANES), F32)]
            + [pltpu.VMEM((total, LANES), F32)] * 4
            + [
                pltpu.VMEM((rows, 2 * channels), BF16),
                pltpu.VMEM((total, inner), BF16),
                pltpu.VMEM((RING * RING, depth, 2 * channels), BF16),
                pltpu.SemaphoreType.DMA((2 * RING * RING + 3,)),
            ],
        ),
        out_shape=[
            shape((rows, channels), BF16),
            shape((2, channels, rows), BF16),
            shape((rows, inner), BF16),
            shape((2, RING, channels, depth), BF16),
            shape((tall, channels), F32),
        ],
        compiler_params=pltpu.CompilerParams(vmem_limit_bytes=60 * MIB),
        cost_estimate=pl.CostEstimate(
            flops=40 * 10**9, bytes_accessed=40 * MIB, transcendentals=0
        ),
    )(place, *pieces, *parts, gout, taps)


def weight_body(order, grad, a, b, c, d, out):
    for q, part in enumerate((a, b, c, d)):
        out[0, q] = jnp.dot(grad[0], part[...], preferred_element_type=F32).astype(BF16)


def weight_parts(order, turned_both, whole, depth):
    kinds, channels, rows = turned_both.shape
    count = order.shape[0]

    def block(q):
        return pl.BlockSpec((rows, depth), lambda i, order: (0, order[i, q + 1]))

    return pl.pallas_call(
        weight_body,
        grid_spec=pltpu.PrefetchScalarGridSpec(
            num_scalar_prefetch=1,
            grid=(count,),
            in_specs=[pl.BlockSpec((1, channels, rows), lambda i, order: (order[i, 0], 0, 0))]
            + [block(q) for q in range(RING)],
            out_specs=pl.BlockSpec((1, RING, channels, depth), lambda i, order: (i, 0, 0, 0)),
        ),
        out_shape=jax.ShapeDtypeStruct((count, RING, channels, depth), BF16),
        compiler_params=pltpu.CompilerParams(vmem_limit_bytes=60 * MIB),
        cost_estimate=pl.CostEstimate(
            flops=count * RING * 2 * channels * depth * rows,
            bytes_accessed=count * 4 * MIB,
            transcendentals=0,
        ),
    )(order, turned_both, *[whole] * RING)


def plus(a, *others):
    total = a.astype(F32)
    for other in others:
        total = total + other.astype(F32)
    return total.astype(BF16)


def spread(block, up, down):
    cut = block.shape[0] // 2
    below, above = send(block, up), send(block, down)
    return [block, below, above, send(below[:cut], up), send(above[cut:], down)]


def per_device(frames, w_value, w_gate, taps, grad_out):
    width = taps.shape[0]
    row, col = lax.axis_index("row"), lax.axis_index("col")
    z, y = row // RING, row % RING
    depth = w_value.shape[0]
    turn = way(col % CORES)

    whole = lax.all_gather(frames, "col", axis=1, tiled=True)
    value, gate = spread(w_value, UP_Y, DOWN_Y), spread(w_gate, UP_Z, DOWN_Z)
    grad_out, *near = together(grad_out, *value, *gate)
    value, gate = near[:5], near[5:]
    shape = (RING,) + w_value.shape
    value = jnp.concatenate(value).reshape(shape)
    gate = jnp.concatenate(gate).reshape(shape)
    pieces = spread(value, UP_Z, DOWN_Z) + spread(gate, UP_Y, DOWN_Y)
    before, after = halo(grad_out)
    grad_wide = jnp.concatenate([before, grad_out, after], axis=0)
    before, after = halo(whole)
    place = jnp.stack([z, y, turn]).astype(jnp.int32)
    activated, turned_both, part, first, tap_sum = middle(
        place, pieces, (before, whole, after), grad_wide, taps
    )

    def behind(at, step):
        return (at - step * turn) % RING

    def of_weights(step):
        sides = [1, 2, 3, 4]
        value = [0] + [behind(z, step) * RING + behind(y, q) for q in sides]
        gate = [1] + [behind(z, q) * RING + behind(y, step) for q in sides]
        return [value, gate]

    def table(rows):
        return jnp.array(rows, jnp.int32)

    grad_frames = lax.psum_scatter(part, "col", scatter_dimension=1, tiled=True)

    def folded(stride):
        pairs = [(i, i ^ stride) for i in range(RING * RING)]
        return tap_sum + lax.ppermute(tap_sum, "row", pairs)

    tap_sum = folded(1)
    order = of_weights(2) + of_weights(3) + of_weights(4)
    later = weight_parts(table(order), turned_both, whole, depth)
    later, tap_sum = together(later, tap_sum)

    def shares(step, group):
        cut = slice(2 * group, 2 * group + 2)
        if step == 1:
            return first[0, cut], first[1, cut]
        return later[(step - 2) * 2, cut], later[(step - 2) * 2 + 1, cut]

    def onward(held):
        return send(held[0], ALONG_Z), send(held[1], ALONG_Y)

    moving = [onward(shares(1, 0)), onward(shares(1, 1))]
    last = None
    for step in range(2, RING + 1):
        for group in range(2):
            got = moving[group]
            if last is not None:
                got = together(*got, *last)[:2]
            last = tuple(plus(a, b) for a, b in zip(shares(step, group), got))
            moving[group] = onward(last) if step < RING else last
        if step < RING:
            *last, tap_sum = together(*last, tap_sum)
            tap_sum = folded(2 ** (step - 1))
            tap_sum, *moving[0] = together(tap_sum, *moving[0])
    tap_sum, *moving[0] = together(tap_sum, *moving[0])
    tap_sum = folded(8)
    near = [
        (send(moving[0][kind][0], along), send(moving[0][kind][1], two))
        for kind, along, two in ((0, BACK_Y, TWO_Y), (1, BACK_Z, TWO_Z))
    ]
    grads = []
    for kind, pairs in ((0, ALONG_Y), (1, ALONG_Z)):
        got = send(moving[1][kind][0], pairs)
        grads.append(plus(moving[1][kind][1], *near[kind], got).T)
    return (activated, grad_frames, *grads, tap_sum[:width])


def solution(mesh):
    in_specs = (P("row", "col"), P("row", "col"), P("row", "col"), P(None, "col"), P("row", "col"))
    out_specs = (P("row", "col"), P("row", "col"), P("row", "col"), P("row", "col"), P(None, "col"))
    return jax.shard_map(
        per_device, mesh=mesh, in_specs=in_specs, out_specs=out_specs, check_vma=False
    )
```

time: 394 us -> 223 us (0.57)
  waiting for transfers between devices: 194 us -> 45.5 us
  Pallas kernels: 0 us -> 72.1 us
  blocking collectives: 62.4 us -> 0 us
  matrix products: 57.5 us -> 0 us
  starting transfers between devices: 12.3 us -> 64.1 us
  other arithmetic: 46.2 us -> 7.51 us
  local copies, waits for them, and re-layouts: 4.16 us -> 16.1 us
    all_gather x2 -> x0, waiting for transfers between devices: 94.6 us -> none  [the longest x1 51.9 us: per_device(): lax.all_gather(w_gate, 'row', axis=0, tiled=True)]
    pallas_call x0 -> x2, Pallas kernels: none -> 72.1 us  [the longest x1 58.7 us: middle(): pl.pallas_call(functools.partial(middle_body, width, rows), grid_spec=plt...]
    psum x1 -> x0, blocking collectives: 62.4 us -> none  [per_device(): lax.psum(tap_part.astype(jnp.bfloat16), 'row').astype(jnp.float32)]
    dot_general x5 -> x0, matrix products: 57.5 us -> none  [the longest x1 13 us: per_device(): lax.dot_general(grad_val, full_value, contract, preferred_element_type=jn...]
    ppermute x4 -> x42, starting transfers between devices: 11.9 us -> 64 us  [the longest x34 41.2 us: send(): return lax.ppermute(array, BOTH, pairs)]
    all_gather x1, waiting for transfers between devices: 51.6 us -> 0.01 us  [per_device(): whole = lax.all_gather(frames, 'col', axis=1, tiled=True)]
    reduce_scatter x2 -> x1, waiting for transfers between devices: 37.2 us -> 0.01 us  [per_device(): grad_frames = lax.psum_scatter(part, 'col', scatter_dimension=1, tiled=True)]
    ppermute x4 -> x42, waiting for transfers between devices: 9.03 us -> 44.8 us  [the longest x34 34.4 us: send(): return lax.ppermute(array, BOTH, pairs)]
  transfers between devices with their start and end apart: 9 -> 44, of which waited for: 6 -> 18; matrix products, arithmetic and copies ran while one was open for 13% -> 10% of each run, Pallas kernels for 0% -> 6%
where the time goes in v1:
time: 223 us; the launch traced here: 220 us
  Pallas kernels  72.1 us (32%)
  starting transfers between devices  64.1 us (29%)
  waiting for transfers between devices  45.5 us (20%)
  local copies, waits for them, and re-layouts  16.1 us (7%)
  between operations  14.6 us (7%)
  other arithmetic  7.51 us (3%)
    pallas_call x1, Pallas kernels, middle(): pl.pallas_call(functools.partial(middle_body, width, rows), grid_spec=plt...  58.7 us
    ppermute x34, starting transfers between devices, send(): return lax.ppermute(array, BOTH, pairs)  41.2 us
    ppermute x34, waiting for transfers between devices, send(): return lax.ppermute(array, BOTH, pairs)  34.4 us
    pallas_call x1, Pallas kernels, weight_parts(): pl.pallas_call(weight_body, grid_spec=pltpu.PrefetchScalarGridSpec(num_sc...  13.4 us
    ppermute x4, starting transfers between devices, folded(): return tap_sum + lax.ppermute(tap_sum, 'row', pairs)  9.63 us
    ppermute x2, starting transfers between devices, halo(): after = lax.ppermute(array[:EDGE], 'row', down)  8.65 us
    unnamed x30, local copies, waits for them, and re-layouts  8.06 us
    ppermute x4, waiting for transfers between devices, folded(): return tap_sum + lax.ppermute(tap_sum, 'row', pairs)  7.79 us
  transfers between devices with their start and end apart: 44, of which 18 were waited for; matrix products, arithmetic and copies ran while one was open for 10% of the time, Pallas kernels for 6%

profile of v1, /device:TPU:42, one launch (start us, length us, event | category | flops | bytes accessed | tf_op | source)
XLA Modules:
  0.0 219.9 jit_solution(5113202744563826484)
XLA Ops:
  7.2 0.7 all-gather.2.cloned.1.call-update
  8.0 1.6 collective-permute-start
  10.1 1.9 collective-permute-start.4
  12.1 4.2 %collective-permute-done = bf16[256,512]{1,0:T(8,128)(2,1)S(1)} collective-permute-done((bf16[256,512]{1,0:T(8,128)(2,1)}, bf16[256,512]{1,0:T(8,128)(2,1)S(1)}, u32[]{:S(2)}, u32[]{:S(2)}) %collective-permute-start) | collective-permute-done | bytes 262176 | tf_op jit(solution)/shard_map/ppermute | solution.py:50
  16.3 1.6 collective-permute-start.2
  18.5 2.0 collective-permute-start.6
  21.3 1.7 collective-permute-done.3
  23.6 2.0 collective-permute-done.7
  25.6 0.7 constant_dynamic-update-slice_fusion.9
  26.3 0.7 constant_dynamic-update-slice_fusion.8
  27.0 0.7 constant_dynamic-update-slice_fusion.7
  27.7 0.7 constant_dynamic-update-slice_fusion.6
  29.0 1.6 collective-permute-start.12
  30.6 1.4 collective-permute-start.13
  32.0 0.7 constant_dynamic-update-slice_fusion.4
  32.7 0.7 constant_dynamic-update-slice_fusion.3
  33.4 0.7 constant_dynamic-update-slice_fusion.2
  34.1 0.7 constant_dynamic-update-slice_fusion.1
  34.8 0.7 constant_dynamic-update-slice_fusion
  35.5 1.6 collective-permute-start.8
  38.1 2.6 %collective-permute-start.18 = (bf16[32,512]{1,0:T(8,128)(2,1)S(1)}, bf16[32,512]{1,0:T(8,128)(2,1)S(1)}, u32[]{:S(2)}, u32[]{:S(2)}) collective-permute-start(bf16[32,512]{1,0:T(8,128)(2,1)S(1)} %get-tuple-element.106), channel_id=1, source_target_pairs={{0,8},{8,16},{16,24},{24,32},{32,40},{40,48},{48,56},{56,64},{64,7... | collective-permute-start | bytes 98312 | tf_op jit(solution)/shard_map/ppermute | solution.py:57
  40.7 0.7 pad_add_fusion.place
  41.4 11.9 %collective-permute-done.12.refs_6_ = bf16[4,256,512]{2,1,0:T(8,128)(2,1)S(1)} collective-permute-done((bf16[4,256,512]{2,1,0:T(8,128)(2,1)}, bf16[4,256,512]{2,1,0:T(8,128)(2,1)S(1)}, u32[]{:S(2)}, u32[]{:S(2)}) %collective-permute-start.12) | collective-permute-done | bytes 1048608 | tf_op jit(solution)/shard_map/ppermute | solution.py:50
  53.3 4.9 %collective-permute-start.19 = (bf16[32,512]{1,0:T(8,128)(2,1)S(1)}, bf16[32,512]{1,0:T(8,128)(2,1)S(1)}, u32[]{:S(2)}, u32[]{:S(2)}) collective-permute-start(bf16[32,512]{1,0:T(8,128)(2,1)S(1)} %get-tuple-element.107), channel_id=1, source_target_pairs={{8,0},{16,8},{24,16},{32,24},{40,32},{48,40},{56,48},{64,56},{72,6... | collective-permute-start | bytes 98312 | tf_op jit(solution)/shard_map/ppermute | solution.py:58
  58.3 1.1 slice.155
  59.4 2.3 %collective-permute-start.15 = (bf16[2,256,512]{2,1,0:T(8,128)(2,1)S(1)}, bf16[2,256,512]{2,1,0:T(8,128)(2,1)}, u32[]{:S(2)}, u32[]{:S(2)}) collective-permute-start(bf16[2,256,512]{2,1,0:T(8,128)(2,1)S(1)} %slice.155), channel_id=1, source_target_pairs={{0,24},{1,25},{2,26},{3,27},{4,28},{5,29},{6,30},{7,31},{8,0},{9,1... | collective-permute-start | bytes 1572872 | tf_op jit(solution)/shard_map/ppermute | solution.py:50
  61.7 1.1 slice.152
  62.8 1.7 collective-permute-start.10
  64.4 1.1 slice.153
  66.0 1.1 fusion.20
  67.1 1.9 collective-permute-start.16
  69.3 3.8 %collective-permute-start.17 = (bf16[32,4096]{1,0:T(8,128)(2,1)S(1)}, bf16[32,4096]{1,0:T(8,128)(2,1)S(1)}, u32[]{:S(2)}, u32[]{:S(2)}) collective-permute-start(bf16[32,4096]{1,0:T(8,128)(2,1)S(1)} %get-tuple-element.88), channel_id=1, source_target_pairs={{8,0},{16,8},{24,16},{32,24},{40,32},{48,40},{56,48},{64,56},{72,6... | collective-permute-start | bytes 786440 | tf_op jit(solution)/shard_map/ppermute | solution.py:58
  73.1 1.1 pad_maximum_fusion.refs_13_
  74.2 0.7 collective-permute-done.11.refs_4_
  75.4 2.2 %collective-permute-done.17.refs_12_ = bf16[32,4096]{1,0:T(8,128)(2,1)S(1)} collective-permute-done((bf16[32,4096]{1,0:T(8,128)(2,1)S(1)}, bf16[32,4096]{1,0:T(8,128)(2,1)S(1)}, u32[]{:S(2)}, u32[]{:S(2)}) %collective-permute-start.17) | collective-permute-done | bytes 262176 | tf_op jit(solution)/shard_map/ppermute | solution.py:58
  77.6 0.7 copy-done.9
  78.3 58.7 %shard_map.92 = (bf16[1024,512]{1,0:T(8,128)(2,1)}, bf16[2,512,1024]{2,1,0:T(8,128)(2,1)}, bf16[1024,4096]{1,0:T(8,128)(2,1)}, bf16[2,4,512,256]{3,2,1,0:T(8,128)(2,1)}, f32[32,512]{1,0:T(8,128)}) custom-call(s32[3]{0:T(128)} %pad_add_fusion.place, bf16[4,256,512]{2,1,0:T(8,128)(2,1)} %bitcast.3.refs_0_, ...), custom_call_target="tpu_custom_call" | custom-call | flops 40000000000 | bytes 41943040 | tf_op jit(solution)/shard_map/pallas_call | solution.py:232
  138.3 2.4 %collective-permute-start.20 = (f32[32,512]{1,0:T(8,128)S(1)}, f32[32,512]{1,0:T(8,128)S(1)}, u32[]{:S(2)}, u32[]{:S(2)}) collective-permute-start(f32[32,512]{1,0:T(8,128)S(1)} %copy-done.6), channel_id=1, source_target_pairs={{0,8},{8,0},{16,24},{24,16},{32,40},{40,32},{48,56},{56,48},{64,72... | collective-permute-start | bytes 196616 | tf_op jit(solution)/shard_map/ppermute | solution.py:351
  140.7 1.1 slice_bitcast_fusion
  141.8 1.6 collective-permute-start.23
  143.4 3.6 %collective-permute-start.24 = (bf16[2,512,256]{2,1,0:T(8,128)(2,1)}, bf16[2,512,256]{2,1,0:T(8,128)(2,1)S(1)}, u32[]{:S(2)}, u32[]{:S(2)}) collective-permute-start(bf16[2,512,256]{2,1,0:T(8,128)(2,1)} %get-tuple-element.102), channel_id=1, source_target_pairs={{0,8},{1,25},{2,10},{3,27},{4,12},{5,29},{6,14},{7,31},{8,16},{9,1... | collective-permute-start | bytes 1572872 | tf_op jit(solution)/shard_map/ppermute | solution.py:50
  147.3 13.4 %shard_map.93 = bf16[6,4,512,256]{3,2,1,0:T(8,128)(2,1)} custom-call(s32[6,5]{1,0:T(8,128)} %concatenate.39.order, bf16[2,512,1024]{2,1,0:T(8,128)(2,1)} %get-tuple-element.57.grad, bf16[1024,4096]{1,0:T(8,128)(2,1)} %all-gather.2.cloned.1.call-done.refs_11_.a.b.c.d, bf16[1024,4096]{1,0:T(8,128)(2,1)} %all-gather.2.cloned.1.call-done.refs_11_.a.b.c.d, ...), custom_call_target="tpu_custom_call" | custom-call | flops 6442450944 | bytes 25165824 | tf_op jit(solution)/shard_map/pallas_call | solution.py:280
  160.8 1.6 fusion.7
  162.4 2.1 collective-permute-start.28
  165.1 1.5 fusion.6
  166.6 1.7 collective-permute-start.25
  168.3 3.8 %collective-permute-start.27 = (f32[32,512]{1,0:T(8,128)S(1)}, f32[32,512]{1,0:T(8,128)S(1)}, u32[]{:S(2)}, u32[]{:S(2)}) collective-permute-start(f32[32,512]{1,0:T(8,128)S(1)} %add.221), channel_id=1, source_target_pairs={{0,16},{8,24},{16,0},{24,8},{32,48},{40,56},{48,32},{56,40},{64,80... | collective-permute-start | bytes 196616 | tf_op jit(solution)/shard_map/ppermute | solution.py:351
  172.1 3.0 %collective-permute-done.27 = f32[32,512]{1,0:T(8,128)S(1)} collective-permute-done((f32[32,512]{1,0:T(8,128)S(1)}, f32[32,512]{1,0:T(8,128)S(1)}, u32[]{:S(2)}, u32[]{:S(2)}) %collective-permute-start.27) | collective-permute-done | bytes 65568 | tf_op jit(solution)/shard_map/ppermute | solution.py:351
  175.4 1.2 collective-permute-start.33
  176.6 1.9 collective-permute-start.34
  179.0 2.3 %collective-permute-done.26 = bf16[2,512,256]{2,1,0:T(8,128)(2,1)S(1)} collective-permute-done((bf16[2,512,256]{2,1,0:T(8,128)(2,1)S(1)}, bf16[2,512,256]{2,1,0:T(8,128)(2,1)S(1)}, u32[]{:S(2)}, u32[]{:S(2)}) %collective-permute-start.26) | collective-permute-done | bytes 524320 | tf_op jit(solution)/shard_map/ppermute | solution.py:50
  181.5 0.8 collective-permute-start.32
  182.3 1.7 collective-permute-start.30
  184.0 4.8 %collective-permute-done.32 = f32[32,512]{1,0:T(8,128)S(1)} collective-permute-done((f32[32,512]{1,0:T(8,128)S(1)}, f32[32,512]{1,0:T(8,128)S(1)}, u32[]{:S(2)}, u32[]{:S(2)}) %collective-permute-start.32) | collective-permute-done | bytes 65568 | tf_op jit(solution)/shard_map/ppermute | solution.py:351
  189.1 2.7 %collective-permute-start.41 = (f32[32,512]{1,0:T(8,128)S(1)}, f32[32,512]{1,0:T(8,128)S(1)}, u32[]{:S(2)}, u32[]{:S(2)}) collective-permute-start(f32[32,512]{1,0:T(8,128)S(1)} %add.231), channel_id=1, source_target_pairs={{0,64},{8,72},{16,80},{24,88},{32,96},{40,104},{48,112},{56,120},{... | collective-permute-start | bytes 196616 | tf_op jit(solution)/shard_map/ppermute | solution.py:351
  192.0 1.1 collective-permute-start.39
  193.1 4.2 %collective-permute-done.30 = bf16[2,512,256]{2,1,0:T(8,128)(2,1)S(1)} collective-permute-done((bf16[2,512,256]{2,1,0:T(8,128)(2,1)S(1)}, bf16[2,512,256]{2,1,0:T(8,128)(2,1)S(1)}, u32[]{:S(2)}, u32[]{:S(2)}) %collective-permute-start.30) | collective-permute-done | bytes 524320 | tf_op jit(solution)/shard_map/ppermute | solution.py:50
  198.3 1.6 collective-permute-start.40
  199.9 4.2 %collective-permute-start.35 = (bf16[512,256]{1,0:T(8,128)(2,1)S(1)}, bf16[512,256]{1,0:T(8,128)(2,1)S(1)}, u32[]{:S(2)}, u32[]{:S(2)}) collective-permute-start(bf16[512,256]{1,0:T(8,128)(2,1)S(1)} %get-tuple-element.110), channel_id=1, source_target_pairs={{0,24},{1,9},{2,26},{3,11},{4,28},{5,13},{6,30},{7,15},{8,0},{9,17... | collective-permute-start | bytes 786440 | tf_op jit(solution)/shard_map/ppermute | solution.py:50
  204.2 1.5 collective-permute-start.37
  206.5 0.8 copy.11
  207.3 0.7 collective-permute-done.35
  208.0 4.1 %collective-permute-done.36 = bf16[512,256]{1,0:T(8,128)(2,1)S(1)} collective-permute-done((bf16[512,256]{1,0:T(8,128)(2,1)S(1)}, bf16[512,256]{1,0:T(8,128)(2,1)S(1)}, u32[]{:S(2)}, u32[]{:S(2)}) %collective-permute-start.36) | collective-permute-done | bytes 262176 | tf_op jit(solution)/shard_map/ppermute | solution.py:50
  212.2 0.8 copy.10
  (97 shorter events, 11.2 us)
Async XLA Ops:
  7.2 24.8 %copy-start.5 = (bf16[256,512]{1,0:T(8,128)(2,1)S(1)}, bf16[256,512]{1,0:T(8,128)(2,1)}, u32[]{:S(2)}) copy-start(bf16[256,512]{1,0:T(8,128)(2,1)} %param.6) | copy-start | bytes 786436
  7.2 18.4 %copy-start.4 = (bf16[256,512]{1,0:T(8,128)(2,1)S(1)}, bf16[256,512]{1,0:T(8,128)(2,1)}, u32[]{:S(2)}) copy-start(bf16[256,512]{1,0:T(8,128)(2,1)} %param.7) | copy-start | bytes 786436
  7.2 58.8 %all-gather.2.cloned.1.call-start = ((), (), s32[]{:S(2)}) async-start(), calls=%async_computation.1 | async-start | bytes 9437184 | tf_op jit(solution)/shard_map/all_gather | solution.py:319
  7.9 205.1 %reduce-scatter.2.cloned.1.call-start = ((), (), s32[]{:S(2)}) async-start(), calls=%async_computation.2 | async-start | bytes 9437184 | tf_op jit(solution)/shard_map/reduce_scatter | solution.py:347
  8.0 8.3 %collective-permute-start = (bf16[256,512]{1,0:T(8,128)(2,1)}, bf16[256,512]{1,0:T(8,128)(2,1)S(1)}, u32[]{:S(2)}, u32[]{:S(2)}) collective-permute-start(bf16[256,512]{1,0:T(8,128)(2,1)} %param.6), channel_id=1, source_target_pairs={{0,8},{1,9},{2,10},{3,11},{4,12},{5,13},{6,14},{7,15},{8,16},{9,17... | collective-permute-start | bytes 786440 | tf_op jit(solution)/shard_map/ppermute | solution.py:50
  9.6 8.3 %collective-permute-start.1 = (bf16[256,512]{1,0:T(8,128)(2,1)}, bf16[256,512]{1,0:T(8,128)(2,1)S(1)}, u32[]{:S(2)}, u32[]{:S(2)}) collective-permute-start(bf16[256,512]{1,0:T(8,128)(2,1)} %param.6), channel_id=1, source_target_pairs={{0,24},{1,25},{2,26},{3,27},{4,28},{5,29},{6,30},{7,31},{8,0},{9,1... | collective-permute-start | bytes 786440 | tf_op jit(solution)/shard_map/ppermute | solution.py:50
  10.1 8.4 %collective-permute-start.4 = (bf16[256,512]{1,0:T(8,128)(2,1)}, bf16[256,512]{1,0:T(8,128)(2,1)S(1)}, u32[]{:S(2)}, u32[]{:S(2)}) collective-permute-start(bf16[256,512]{1,0:T(8,128)(2,1)} %param.7), channel_id=1, source_target_pairs={{0,32},{1,33},{2,34},{3,35},{4,36},{5,37},{6,38},{7,39},{8,40},{9,... | collective-permute-start | bytes 786440 | tf_op jit(solution)/shard_map/ppermute | solution.py:50
  12.0 8.5 %collective-permute-start.5 = (bf16[256,512]{1,0:T(8,128)(2,1)}, bf16[256,512]{1,0:T(8,128)(2,1)S(1)}, u32[]{:S(2)}, u32[]{:S(2)}) collective-permute-start(bf16[256,512]{1,0:T(8,128)(2,1)} %param.7), channel_id=1, source_target_pairs={{0,96},{1,97},{2,98},{3,99},{4,100},{5,101},{6,102},{7,103},{8,104... | collective-permute-start | bytes 786440 | tf_op jit(solution)/shard_map/ppermute | solution.py:50
  16.3 5.0 %collective-permute-start.2 = (bf16[128,512]{1,0:T(8,128)(2,1)S(1)}, bf16[128,512]{1,0:T(8,128)(2,1)S(1)}, u32[]{:S(2)}, u32[]{:S(2)}) collective-permute-start(bf16[128,512]{1,0:T(8,128)(2,1)S(1)} %slice.148), channel_id=1, source_target_pairs={{0,8},{1,9},{2,10},{3,11},{4,12},{5,13},{6,14},{7,15},{8,16},{9,17... | collective-permute-start | bytes 393224 | tf_op jit(solution)/shard_map/ppermute | solution.py:50
  18.0 5.0 %collective-permute-start.3 = (bf16[128,512]{1,0:T(8,128)(2,1)S(1)}, bf16[128,512]{1,0:T(8,128)(2,1)S(1)}, u32[]{:S(2)}, u32[]{:S(2)}) collective-permute-start(bf16[128,512]{1,0:T(8,128)(2,1)S(1)} %slice.149), channel_id=1, source_target_pairs={{0,24},{1,25},{2,26},{3,27},{4,28},{5,29},{6,30},{7,31},{8,0},{9,1... | collective-permute-start | bytes 393224 | tf_op jit(solution)/shard_map/ppermute | solution.py:50
  18.5 19.0 %copy-start.7 = (bf16[31,512]{1,0:T(8,128)(2,1)S(1)}, bf16[31,512]{1,0:T(8,128)(2,1)}, u32[]{:S(2)}) copy-start(bf16[31,512]{1,0:T(8,128)(2,1)} %param.8) | copy-start | bytes 95236
  18.5 5.0 %collective-permute-start.6 = (bf16[128,512]{1,0:T(8,128)(2,1)S(1)}, bf16[128,512]{1,0:T(8,128)(2,1)S(1)}, u32[]{:S(2)}, u32[]{:S(2)}) collective-permute-start(bf16[128,512]{1,0:T(8,128)(2,1)S(1)} %slice.150), channel_id=1, source_target_pairs={{0,32},{1,33},{2,34},{3,35},{4,36},{5,37},{6,38},{7,39},{8,40},{9,... | collective-permute-start | bytes 393224 | tf_op jit(solution)/shard_map/ppermute | solution.py:50
  20.5 17.6 %copy-start.2 = (bf16[1024,512]{1,0:T(8,128)(2,1)S(1)}, bf16[1024,512]{1,0:T(8,128)(2,1)}, u32[]{:S(2)}) copy-start(bf16[1024,512]{1,0:T(8,128)(2,1)} %param.9) | copy-start | bytes 3145732
  20.5 5.0 %collective-permute-start.7 = (bf16[128,512]{1,0:T(8,128)(2,1)S(1)}, bf16[128,512]{1,0:T(8,128)(2,1)S(1)}, u32[]{:S(2)}, u32[]{:S(2)}) collective-permute-start(bf16[128,512]{1,0:T(8,128)(2,1)S(1)} %slice.151), channel_id=1, source_target_pairs={{0,96},{1,97},{2,98},{3,99},{4,100},{5,101},{6,102},{7,103},{8,104... | collective-permute-start | bytes 393224 | tf_op jit(solution)/shard_map/ppermute | solution.py:50
  29.0 24.3 %collective-permute-start.12 = (bf16[4,256,512]{2,1,0:T(8,128)(2,1)}, bf16[4,256,512]{2,1,0:T(8,128)(2,1)S(1)}, u32[]{:S(2)}, u32[]{:S(2)}) collective-permute-start(bf16[4,256,512]{2,1,0:T(8,128)(2,1)} %bitcast.4.refs_5_), channel_id=1, source_target_pairs={{0,8},{1,9},{2,10},{3,11},{4,12},{5,13},{6,14},{7,15},{8,16},{9,17... | collective-permute-start | bytes 3145736 | tf_op jit(solution)/shard_map/ppermute | solution.py:50
  30.6 27.6 %collective-permute-start.13 = (bf16[4,256,512]{2,1,0:T(8,128)(2,1)}, bf16[4,256,512]{2,1,0:T(8,128)(2,1)}, u32[]{:S(2)}, u32[]{:S(2)}) collective-permute-start(bf16[4,256,512]{2,1,0:T(8,128)(2,1)} %bitcast.4.refs_5_), channel_id=1, source_target_pairs={{0,24},{1,25},{2,26},{3,27},{4,28},{5,29},{6,30},{7,31},{8,0},{9,1... | collective-permute-start | bytes 3145736 | tf_op jit(solution)/shard_map/ppermute | solution.py:50
  35.5 23.9 %collective-permute-start.8 = (bf16[4,256,512]{2,1,0:T(8,128)(2,1)}, bf16[4,256,512]{2,1,0:T(8,128)(2,1)}, u32[]{:S(2)}, u32[]{:S(2)}) collective-permute-start(bf16[4,256,512]{2,1,0:T(8,128)(2,1)} %bitcast.3.refs_0_), channel_id=1, source_target_pairs={{0,32},{1,33},{2,34},{3,35},{4,36},{5,37},{6,38},{7,39},{8,40},{9,... | collective-permute-start | bytes 3145736 | tf_op jit(solution)/shard_map/ppermute | solution.py:50
  37.1 25.7 %collective-permute-start.9 = (bf16[4,256,512]{2,1,0:T(8,128)(2,1)}, bf16[4,256,512]{2,1,0:T(8,128)(2,1)}, u32[]{:S(2)}, u32[]{:S(2)}) collective-permute-start(bf16[4,256,512]{2,1,0:T(8,128)(2,1)} %bitcast.3.refs_0_), channel_id=1, source_target_pairs={{0,96},{1,97},{2,98},{3,99},{4,100},{5,101},{6,102},{7,103},{8,104... | collective-permute-start | bytes 3145736 | tf_op jit(solution)/shard_map/ppermute | solution.py:50
  38.1 27.4 %collective-permute-start.18 = (bf16[32,512]{1,0:T(8,128)(2,1)S(1)}, bf16[32,512]{1,0:T(8,128)(2,1)S(1)}, u32[]{:S(2)}, u32[]{:S(2)}) collective-permute-start(bf16[32,512]{1,0:T(8,128)(2,1)S(1)} %get-tuple-element.106), channel_id=1, source_target_pairs={{0,8},{8,16},{16,24},{24,32},{32,40},{40,48},{48,56},{56,64},{64,7... | collective-permute-start | bytes 98312 | tf_op jit(solution)/shard_map/ppermute | solution.py:57
  53.3 6.1 %copy-start.3 = (bf16[4,256,512]{2,1,0:T(8,128)(2,1)}, bf16[4,256,512]{2,1,0:T(8,128)(2,1)S(1)}, u32[]{:S(2)}) copy-start(bf16[4,256,512]{2,1,0:T(8,128)(2,1)S(1)} %collective-permute-done.12.refs_6_) | copy-start | bytes 3145732
  53.3 13.8 %collective-permute-start.19 = (bf16[32,512]{1,0:T(8,128)(2,1)S(1)}, bf16[32,512]{1,0:T(8,128)(2,1)S(1)}, u32[]{:S(2)}, u32[]{:S(2)}) collective-permute-start(bf16[32,512]{1,0:T(8,128)(2,1)S(1)} %get-tuple-element.107), channel_id=1, source_target_pairs={{8,0},{16,8},{24,16},{32,24},{40,32},{48,40},{56,48},{64,56},{72,6... | collective-permute-start | bytes 98312 | tf_op jit(solution)/shard_map/ppermute | solution.py:58
  58.2 11.1 %collective-permute-start.14 = (bf16[2,256,512]{2,1,0:T(8,128)(2,1)S(1)}, bf16[2,256,512]{2,1,0:T(8,128)(2,1)}, u32[]{:S(2)}, u32[]{:S(2)}) collective-permute-start(bf16[2,256,512]{2,1,0:T(8,128)(2,1)S(1)} %slice.154), channel_id=1, source_target_pairs={{0,8},{1,9},{2,10},{3,11},{4,12},{5,13},{6,14},{7,15},{8,16},{9,17... | collective-permute-start | bytes 1572872 | tf_op jit(solution)/shard_map/ppermute | solution.py:50
  59.4 14.8 %collective-permute-start.15 = (bf16[2,256,512]{2,1,0:T(8,128)(2,1)S(1)}, bf16[2,256,512]{2,1,0:T(8,128)(2,1)}, u32[]{:S(2)}, u32[]{:S(2)}) collective-permute-start(bf16[2,256,512]{2,1,0:T(8,128)(2,1)S(1)} %slice.155), channel_id=1, source_target_pairs={{0,24},{1,25},{2,26},{3,27},{4,28},{5,29},{6,30},{7,31},{8,0},{9,1... | collective-permute-start | bytes 1572872 | tf_op jit(solution)/shard_map/ppermute | solution.py:50
  62.8 11.5 %collective-permute-start.10 = (bf16[2,256,512]{2,1,0:T(8,128)(2,1)S(1)}, bf16[2,256,512]{2,1,0:T(8,128)(2,1)}, u32[]{:S(2)}, u32[]{:S(2)}) collective-permute-start(bf16[2,256,512]{2,1,0:T(8,128)(2,1)S(1)} %slice.152), channel_id=1, source_target_pairs={{0,32},{1,33},{2,34},{3,35},{4,36},{5,37},{6,38},{7,39},{8,40},{9,... | collective-permute-start | bytes 1572872 | tf_op jit(solution)/shard_map/ppermute | solution.py:50
  65.5 9.4 %collective-permute-start.11 = (bf16[2,256,512]{2,1,0:T(8,128)(2,1)S(1)}, bf16[2,256,512]{2,1,0:T(8,128)(2,1)}, u32[]{:S(2)}, u32[]{:S(2)}) collective-permute-start(bf16[2,256,512]{2,1,0:T(8,128)(2,1)S(1)} %slice.153), channel_id=1, source_target_pairs={{0,96},{1,97},{2,98},{3,99},{4,100},{5,101},{6,102},{7,103},{8,104... | collective-permute-start | bytes 1572872 | tf_op jit(solution)/shard_map/ppermute | solution.py:50
  67.1 8.3 %collective-permute-start.16 = (bf16[32,4096]{1,0:T(8,128)(2,1)S(1)}, bf16[32,4096]{1,0:T(8,128)(2,1)S(1)}, u32[]{:S(2)}, u32[]{:S(2)}) collective-permute-start(bf16[32,4096]{1,0:T(8,128)(2,1)S(1)} %get-tuple-element.89), channel_id=1, source_target_pairs={{0,8},{8,16},{16,24},{24,32},{32,40},{40,48},{48,56},{56,64},{64,7... | collective-permute-start | bytes 786440 | tf_op jit(solution)/shard_map/ppermute | solution.py:57
  69.3 8.3 %collective-permute-start.17 = (bf16[32,4096]{1,0:T(8,128)(2,1)S(1)}, bf16[32,4096]{1,0:T(8,128)(2,1)S(1)}, u32[]{:S(2)}, u32[]{:S(2)}) collective-permute-start(bf16[32,4096]{1,0:T(8,128)(2,1)S(1)} %get-tuple-element.88), channel_id=1, source_target_pairs={{8,0},{16,8},{24,16},{32,24},{40,32},{48,40},{56,48},{64,56},{72,6... | collective-permute-start | bytes 786440 | tf_op jit(solution)/shard_map/ppermute | solution.py:58
  75.4 2.2 %copy-start.8 = (bf16[32,4096]{1,0:T(8,128)(2,1)}, bf16[32,4096]{1,0:T(8,128)(2,1)S(1)}, u32[]{:S(2)}) copy-start(bf16[32,4096]{1,0:T(8,128)(2,1)S(1)} %collective-permute-done.16.refs_10_) | copy-start | bytes 786436
  77.6 0.7 copy-start.9
  137.0 1.3 copy-start.6
  137.0 3.7 %copy-start.1 = (bf16[2,4,512,256]{3,2,1,0:T(8,128)(2,1)S(1)}, bf16[2,4,512,256]{3,2,1,0:T(8,128)(2,1)}, u32[]{:S(2)}) copy-start(bf16[2,4,512,256]{3,2,1,0:T(8,128)(2,1)} %get-tuple-element.60) | copy-start | bytes 6291460
  138.3 22.5 %collective-permute-start.20 = (f32[32,512]{1,0:T(8,128)S(1)}, f32[32,512]{1,0:T(8,128)S(1)}, u32[]{:S(2)}, u32[]{:S(2)}) collective-permute-start(f32[32,512]{1,0:T(8,128)S(1)} %copy-done.6), channel_id=1, source_target_pairs={{0,8},{8,0},{16,24},{24,16},{32,40},{40,32},{48,56},{56,48},{64,72... | collective-permute-start | bytes 196616 | tf_op jit(solution)/shard_map/ppermute | solution.py:351
  141.8 19.0 %collective-permute-start.23 = (bf16[2,512,256]{2,1,0:T(8,128)(2,1)}, bf16[2,512,256]{2,1,0:T(8,128)(2,1)S(1)}, u32[]{:S(2)}, u32[]{:S(2)}) collective-permute-start(bf16[2,512,256]{2,1,0:T(8,128)(2,1)} %get-tuple-element.103), channel_id=1, source_target_pairs={{0,32},{1,97},{2,34},{3,99},{4,36},{5,101},{6,38},{7,103},{8,40},{... | collective-permute-start | bytes 1572872 | tf_op jit(solution)/shard_map/ppermute | solution.py:50
  143.4 17.4 %collective-permute-start.24 = (bf16[2,512,256]{2,1,0:T(8,128)(2,1)}, bf16[2,512,256]{2,1,0:T(8,128)(2,1)S(1)}, u32[]{:S(2)}, u32[]{:S(2)}) collective-permute-start(bf16[2,512,256]{2,1,0:T(8,128)(2,1)} %get-tuple-element.102), channel_id=1, source_target_pairs={{0,8},{1,25},{2,10},{3,27},{4,12},{5,29},{6,14},{7,31},{8,16},{9,1... | collective-permute-start | bytes 1572872 | tf_op jit(solution)/shard_map/ppermute | solution.py:50
  147.0 18.1 %collective-permute-start.21 = (bf16[2,512,256]{2,1,0:T(8,128)(2,1)S(1)}, bf16[2,512,256]{2,1,0:T(8,128)(2,1)S(1)}, u32[]{:S(2)}, u32[]{:S(2)}) collective-permute-start(bf16[2,512,256]{2,1,0:T(8,128)(2,1)S(1)} %get-tuple-element.105), channel_id=1, source_target_pairs={{0,32},{1,97},{2,34},{3,99},{4,36},{5,101},{6,38},{7,103},{8,40},{... | collective-permute-start | bytes 1572872 | tf_op jit(solution)/shard_map/ppermute | solution.py:50
  147.0 18.1 %collective-permute-start.22 = (bf16[2,512,256]{2,1,0:T(8,128)(2,1)S(1)}, bf16[2,512,256]{2,1,0:T(8,128)(2,1)S(1)}, u32[]{:S(2)}, u32[]{:S(2)}) collective-permute-start(bf16[2,512,256]{2,1,0:T(8,128)(2,1)S(1)} %get-tuple-element.104), channel_id=1, source_target_pairs={{0,8},{1,25},{2,10},{3,27},{4,12},{5,29},{6,14},{7,31},{8,16},{9,1... | collective-permute-start | bytes 1572872 | tf_op jit(solution)/shard_map/ppermute | solution.py:50
  160.8 14.3 %copy-start = (bf16[6,4,512,256]{3,2,1,0:T(8,128)(2,1)S(1)}, bf16[6,4,512,256]{3,2,1,0:T(8,128)(2,1)}, u32[]{:S(2)}) copy-start(bf16[6,4,512,256]{3,2,1,0:T(8,128)(2,1)} %shard_map.93) | copy-start | bytes 18874372
  162.4 12.7 %collective-permute-start.28 = (bf16[2,512,256]{2,1,0:T(8,128)(2,1)S(1)}, bf16[2,512,256]{2,1,0:T(8,128)(2,1)S(1)}, u32[]{:S(2)}, u32[]{:S(2)}) collective-permute-start(bf16[2,512,256]{2,1,0:T(8,128)(2,1)S(1)} %get-tuple-element.101), channel_id=1, source_target_pairs={{0,32},{1,97},{2,34},{3,99},{4,36},{5,101},{6,38},{7,103},{8,40},{... | collective-permute-start | bytes 1572872 | tf_op jit(solution)/shard_map/ppermute | solution.py:50
  164.6 10.6 %collective-permute-start.29 = (bf16[2,512,256]{2,1,0:T(8,128)(2,1)S(1)}, bf16[2,512,256]{2,1,0:T(8,128)(2,1)S(1)}, u32[]{:S(2)}, u32[]{:S(2)}) collective-permute-start(bf16[2,512,256]{2,1,0:T(8,128)(2,1)S(1)} %get-tuple-element.100), channel_id=1, source_target_pairs={{0,8},{1,25},{2,10},{3,27},{4,12},{5,29},{6,14},{7,31},{8,16},{9,1... | collective-permute-start | bytes 1572872 | tf_op jit(solution)/shard_map/ppermute | solution.py:50
  166.6 12.4 %collective-permute-start.25 = (bf16[2,512,256]{2,1,0:T(8,128)(2,1)S(1)}, bf16[2,512,256]{2,1,0:T(8,128)(2,1)S(1)}, u32[]{:S(2)}, u32[]{:S(2)}) collective-permute-start(bf16[2,512,256]{2,1,0:T(8,128)(2,1)S(1)} %get-tuple-element.99), channel_id=1, source_target_pairs={{0,32},{1,97},{2,34},{3,99},{4,36},{5,101},{6,38},{7,103},{8,40},{... | collective-permute-start | bytes 1572872 | tf_op jit(solution)/shard_map/ppermute | solution.py:50
  168.3 6.8 %collective-permute-start.27 = (f32[32,512]{1,0:T(8,128)S(1)}, f32[32,512]{1,0:T(8,128)S(1)}, u32[]{:S(2)}, u32[]{:S(2)}) collective-permute-start(f32[32,512]{1,0:T(8,128)S(1)} %add.221), channel_id=1, source_target_pairs={{0,16},{8,24},{16,0},{24,8},{32,48},{40,56},{48,32},{56,40},{64,80... | collective-permute-start | bytes 196616 | tf_op jit(solution)/shard_map/ppermute | solution.py:351
  172.1 9.2 %collective-permute-start.26 = (bf16[2,512,256]{2,1,0:T(8,128)(2,1)S(1)}, bf16[2,512,256]{2,1,0:T(8,128)(2,1)S(1)}, u32[]{:S(2)}, u32[]{:S(2)}) collective-permute-start(bf16[2,512,256]{2,1,0:T(8,128)(2,1)S(1)} %get-tuple-element.98), channel_id=1, source_target_pairs={{0,8},{1,25},{2,10},{3,27},{4,12},{5,29},{6,14},{7,31},{8,16},{9,1... | collective-permute-start | bytes 1572872 | tf_op jit(solution)/shard_map/ppermute | solution.py:50
  175.4 13.4 %collective-permute-start.33 = (bf16[2,512,256]{2,1,0:T(8,128)(2,1)S(1)}, bf16[2,512,256]{2,1,0:T(8,128)(2,1)S(1)}, u32[]{:S(2)}, u32[]{:S(2)}) collective-permute-start(bf16[2,512,256]{2,1,0:T(8,128)(2,1)S(1)} %get-tuple-element.97), channel_id=1, source_target_pairs={{0,32},{1,97},{2,34},{3,99},{4,36},{5,101},{6,38},{7,103},{8,40},{... | collective-permute-start | bytes 1572872 | tf_op jit(solution)/shard_map/ppermute | solution.py:50
  176.6 12.2 %collective-permute-start.34 = (bf16[2,512,256]{2,1,0:T(8,128)(2,1)S(1)}, bf16[2,512,256]{2,1,0:T(8,128)(2,1)S(1)}, u32[]{:S(2)}, u32[]{:S(2)}) collective-permute-start(bf16[2,512,256]{2,1,0:T(8,128)(2,1)S(1)} %get-tuple-element.96), channel_id=1, source_target_pairs={{0,8},{1,25},{2,10},{3,27},{4,12},{5,29},{6,14},{7,31},{8,16},{9,1... | collective-permute-start | bytes 1572872 | tf_op jit(solution)/shard_map/ppermute | solution.py:50
  181.5 7.2 %collective-permute-start.32 = (f32[32,512]{1,0:T(8,128)S(1)}, f32[32,512]{1,0:T(8,128)S(1)}, u32[]{:S(2)}, u32[]{:S(2)}) collective-permute-start(f32[32,512]{1,0:T(8,128)S(1)} %add.226), channel_id=1, source_target_pairs={{0,32},{8,40},{16,48},{24,56},{32,0},{40,8},{48,16},{56,24},{64,96... | collective-permute-start | bytes 196616 | tf_op jit(solution)/shard_map/ppermute | solution.py:351
  182.3 15.0 %collective-permute-start.30 = (bf16[2,512,256]{2,1,0:T(8,128)(2,1)S(1)}, bf16[2,512,256]{2,1,0:T(8,128)(2,1)S(1)}, u32[]{:S(2)}, u32[]{:S(2)}) collective-permute-start(bf16[2,512,256]{2,1,0:T(8,128)(2,1)S(1)} %get-tuple-element.95), channel_id=1, source_target_pairs={{0,32},{1,97},{2,34},{3,99},{4,36},{5,101},{6,38},{7,103},{8,40},{... | collective-permute-start | bytes 1572872 | tf_op jit(solution)/shard_map/ppermute | solution.py:50
  184.0 14.0 %collective-permute-start.31 = (bf16[2,512,256]{2,1,0:T(8,128)(2,1)S(1)}, bf16[2,512,256]{2,1,0:T(8,128)(2,1)S(1)}, u32[]{:S(2)}, u32[]{:S(2)}) collective-permute-start(bf16[2,512,256]{2,1,0:T(8,128)(2,1)S(1)} %get-tuple-element.94), channel_id=1, source_target_pairs={{0,8},{1,25},{2,10},{3,27},{4,12},{5,29},{6,14},{7,31},{8,16},{9,1... | collective-permute-start | bytes 1572872 | tf_op jit(solution)/shard_map/ppermute | solution.py:50
  189.1 15.0 %collective-permute-start.41 = (f32[32,512]{1,0:T(8,128)S(1)}, f32[32,512]{1,0:T(8,128)S(1)}, u32[]{:S(2)}, u32[]{:S(2)}) collective-permute-start(f32[32,512]{1,0:T(8,128)S(1)} %add.231), channel_id=1, source_target_pairs={{0,64},{8,72},{16,80},{24,88},{32,96},{40,104},{48,112},{56,120},{... | collective-permute-start | bytes 196616 | tf_op jit(solution)/shard_map/ppermute | solution.py:351
  191.8 12.4 %collective-permute-start.38 = (bf16[512,256]{1,0:T(8,128)(2,1)S(1)}, bf16[512,256]{1,0:T(8,128)(2,1)S(1)}, u32[]{:S(2)}, u32[]{:S(2)}) collective-permute-start(bf16[512,256]{1,0:T(8,128)(2,1)S(1)} %get-tuple-element.108), channel_id=1, source_target_pairs={{0,96},{1,33},{2,98},{3,35},{4,100},{5,37},{6,102},{7,39},{8,104},... | collective-permute-start | bytes 786440 | tf_op jit(solution)/shard_map/ppermute | solution.py:50
  192.0 14.3 %collective-permute-start.39 = (bf16[512,256]{1,0:T(8,128)(2,1)S(1)}, bf16[512,256]{1,0:T(8,128)(2,1)S(1)}, u32[]{:S(2)}, u32[]{:S(2)}) collective-permute-start(bf16[512,256]{1,0:T(8,128)(2,1)S(1)} %get-tuple-element.109), channel_id=1, source_target_pairs={{0,64},{1,65},{2,66},{3,67},{4,68},{5,69},{6,70},{7,71},{8,72},{9,... | collective-permute-start | bytes 786440 | tf_op jit(solution)/shard_map/ppermute | solution.py:50
  198.3 8.0 %collective-permute-start.40 = (bf16[512,256]{1,0:T(8,128)(2,1)S(1)}, bf16[512,256]{1,0:T(8,128)(2,1)S(1)}, u32[]{:S(2)}, u32[]{:S(2)}) collective-permute-start(bf16[512,256]{1,0:T(8,128)(2,1)S(1)} %slice_bitcast_fusion.4), channel_id=1, source_target_pairs={{0,32},{1,97},{2,34},{3,99},{4,36},{5,101},{6,38},{7,103},{8,40},{... | collective-permute-start | bytes 786440 | tf_op jit(solution)/shard_map/ppermute | solution.py:50
  199.9 8.1 %collective-permute-start.35 = (bf16[512,256]{1,0:T(8,128)(2,1)S(1)}, bf16[512,256]{1,0:T(8,128)(2,1)S(1)}, u32[]{:S(2)}, u32[]{:S(2)}) collective-permute-start(bf16[512,256]{1,0:T(8,128)(2,1)S(1)} %get-tuple-element.110), channel_id=1, source_target_pairs={{0,24},{1,9},{2,26},{3,11},{4,28},{5,13},{6,30},{7,15},{8,0},{9,17... | collective-permute-start | bytes 786440 | tf_op jit(solution)/shard_map/ppermute | solution.py:50
  204.1 8.0 %collective-permute-start.36 = (bf16[512,256]{1,0:T(8,128)(2,1)S(1)}, bf16[512,256]{1,0:T(8,128)(2,1)S(1)}, u32[]{:S(2)}, u32[]{:S(2)}) collective-permute-start(bf16[512,256]{1,0:T(8,128)(2,1)S(1)} %get-tuple-element.111), channel_id=1, source_target_pairs={{0,16},{1,17},{2,18},{3,19},{4,20},{5,21},{6,22},{7,23},{8,24},{9,... | collective-permute-start | bytes 786440 | tf_op jit(solution)/shard_map/ppermute | solution.py:50
  204.2 7.9 %collective-permute-start.37 = (bf16[512,256]{1,0:T(8,128)(2,1)S(1)}, bf16[512,256]{1,0:T(8,128)(2,1)S(1)}, u32[]{:S(2)}, u32[]{:S(2)}) collective-permute-start(bf16[512,256]{1,0:T(8,128)(2,1)S(1)} %slice_bitcast_fusion.6), channel_id=1, source_target_pairs={{0,8},{1,25},{2,10},{3,27},{4,12},{5,29},{6,14},{7,31},{8,16},{9,1... | collective-permute-start | bytes 786440 | tf_op jit(solution)/shard_map/ppermute | solution.py:50
Sparse Core Ops, SparseCore 0:
  9.7 50.7 all-gather.1
  137.1 54.6 reduce-scatter.1

commit v2 on v1

--- a/solution.py
+++ b/solution.py
@@ -50,13 +50,13 @@
     return lax.ppermute(array, BOTH, pairs)
 
 
-def halo(array):
-    count, length = lax.axis_size("row"), array.shape[0]
+def halo(*arrays):
+    count, length = lax.axis_size("row"), arrays[0].shape[0]
     up = [(i, i + 1) for i in range(count - 1)]
     down = [(j, i) for i, j in up]
-    before = lax.ppermute(array[length - EDGE :], "row", up)
-    after = lax.ppermute(array[:EDGE], "row", down)
-    return before, after
+    last = jnp.concatenate([array[length - EDGE :] for array in arrays], axis=1)
+    first = jnp.concatenate([array[:EDGE] for array in arrays], axis=1)
+    return lax.ppermute(last, "row", up), lax.ppermute(first, "row", down)
 
 
 def together(*values):
@@ -64,19 +64,22 @@
 
 
 def middle_body(width, rows, place, *refs):
-    pieces, (before, inner, after), (gout, taps) = refs[:10], refs[10:13], refs[13:15]
+    pieces, (before, inner, after, grad_out), taps = refs[:10], refs[10:14], refs[14]
     act, turned_both, frames_out, first_out, gtap = refs[15:20]
-    vg, glu, gf, gate_s, vg_s, both, whole, weights, in_sem = refs[20:]
+    vg, glu, gf, gate_s, vg_s, gout, both, whole, weights, in_sem = refs[20:]
     half = (width - 1) // 2
-    total = whole.shape[0]
+    total, width_in = whole.shape
     depth, channels = weights.shape[1], weights.shape[2] // 2
     strip = pl.program_id(0)
     strips = channels // LANES
     z, y, turn = place[0], place[1], place[2]
     copies = [
-        (before, whole.at[pl.ds(0, EDGE), :]),
+        (before.at[:, pl.ds(0, width_in)], whole.at[pl.ds(0, EDGE), :]),
         (inner, whole.at[pl.ds(EDGE, rows), :]),
-        (after, whole.at[pl.ds(EDGE + rows, EDGE), :]),
+        (after.at[:, pl.ds(0, width_in)], whole.at[pl.ds(EDGE + rows, EDGE), :]),
+        (before.at[:, pl.ds(width_in, channels)], gout.at[pl.ds(0, EDGE), :]),
+        (grad_out, gout.at[pl.ds(EDGE, rows), :]),
+        (after.at[:, pl.ds(width_in, channels)], gout.at[pl.ds(EDGE + rows, EDGE), :]),
     ]
     for kind in range(2):
         for far in range(RING):
@@ -119,7 +122,7 @@
             vg_s[at, :] = vp * (1.0 - p)
             return 0
 
-        lax.fori_loop(0, total // STRIP, gates, 0)
+        lax.fori_loop(0, total // STRIP, gates, 0, unroll=2)
         tap = [jnp.broadcast_to(taps[k : k + 1, :], (8, LANES)) for k in range(width)]
 
         def conv(source, start, sign):
@@ -140,11 +143,11 @@
             s = jax.nn.sigmoid(f)
             fs = f * s
             vg[at, :LANES] = fs
-            g = gout[at, :].astype(F32) * (s + fs * (1.0 - s))
+            g = gout[at, pl.ds(pl.multiple_of(strip * LANES, LANES), LANES)].astype(F32) * (s + fs * (1.0 - s))
             gf[at, :] = g.astype(BF16).astype(F32)
             return 0
 
-        lax.fori_loop(0, (rows + EDGE) // STRIP, forward, 0)
+        lax.fori_loop(0, (rows + EDGE) // STRIP, forward, 0, unroll=3)
         act[...] = vg[EDGE : EDGE + rows, :LANES].astype(BF16)
 
         def backward(i, _):
@@ -155,7 +158,7 @@
             vg[at, LANES:] = d * vg_s[at, :]
             return 0
 
-        lax.fori_loop(0, rows // STRIP, backward, 0)
+        lax.fori_loop(0, rows // STRIP, backward, 0, unroll=2)
         for kind in range(2):
             grad = vg[EDGE : EDGE + rows, kind * LANES : (kind + 1) * LANES]
             start = pl.multiple_of(kind * channels + strip * LANES, LANES)
@@ -204,7 +207,7 @@
                 ).astype(BF16)
 
 
-def middle(place, pieces, parts, gout, taps):
+def middle(place, pieces, parts, taps):
     rows, inner = parts[1].shape
     total = rows + 2 * EDGE
     depth, channels = pieces[0].shape[1:]
@@ -234,7 +237,7 @@
         grid_spec=pltpu.PrefetchScalarGridSpec(
             num_scalar_prefetch=1,
             grid=(end + 2,),
-            in_specs=[far() for _ in range(len(pieces) + len(parts))] + [strips(total), strips(tall)],
+            in_specs=[far() for _ in range(len(pieces) + len(parts))] + [strips(tall)],
             out_specs=[
                 strips(rows),
                 pl.BlockSpec((2, channels, rows), lambda j, place: (0, 0, 0)),
@@ -245,10 +248,11 @@
             scratch_shapes=[pltpu.VMEM((total, 2 * LANES), F32)]
             + [pltpu.VMEM((total, LANES), F32)] * 4
             + [
+                pltpu.VMEM((total, channels), BF16),
                 pltpu.VMEM((rows, 2 * channels), BF16),
                 pltpu.VMEM((total, inner), BF16),
                 pltpu.VMEM((RING * RING, depth, 2 * channels), BF16),
-                pltpu.SemaphoreType.DMA((2 * RING * RING + 3,)),
+                pltpu.SemaphoreType.DMA((2 * RING * RING + 6,)),
             ],
         ),
         out_shape=[
@@ -262,7 +266,7 @@
         cost_estimate=pl.CostEstimate(
             flops=40 * 10**9, bytes_accessed=40 * MIB, transcendentals=0
         ),
-    )(place, *pieces, *parts, gout, taps)
+    )(place, *pieces, *parts, taps)
 
 
 def weight_body(order, grad, a, b, c, d, out):
@@ -318,18 +322,16 @@
 
     whole = lax.all_gather(frames, "col", axis=1, tiled=True)
     value, gate = spread(w_value, UP_Y, DOWN_Y), spread(w_gate, UP_Z, DOWN_Z)
-    grad_out, *near = together(grad_out, *value, *gate)
+    near = together(*value, *gate)
     value, gate = near[:5], near[5:]
     shape = (RING,) + w_value.shape
     value = jnp.concatenate(value).reshape(shape)
     gate = jnp.concatenate(gate).reshape(shape)
     pieces = spread(value, UP_Z, DOWN_Z) + spread(gate, UP_Y, DOWN_Y)
-    before, after = halo(grad_out)
-    grad_wide = jnp.concatenate([before, grad_out, after], axis=0)
-    before, after = halo(whole)
+    before, after = halo(whole, grad_out)
     place = jnp.stack([z, y, turn]).astype(jnp.int32)
     activated, turned_both, part, first, tap_sum = middle(
-        place, pieces, (before, whole, after), grad_wide, taps
+        place, pieces, (before, whole, after, grad_out), taps
     )
 
     def behind(at, step):

time: 223 us -> 216 us (0.969); the launches traced: 220 us -> 216 us
  waiting for transfers between devices: 45.5 us -> 56.5 us
  local copies, waits for them, and re-layouts: 16.1 us -> 9.78 us
  starting transfers between devices: 64.1 us -> 60.2 us
  Pallas kernels: 72.1 us -> 68.5 us
    ppermute x4 -> x2, starting transfers between devices: 13.1 us -> 6.02 us  [halo(): return (lax.ppermute(last, 'row', up), lax.ppermute(first, 'row', down))]
    ppermute x34, starting transfers between devices: 41.2 us -> 47.8 us  [send(): return lax.ppermute(array, BOTH, pairs)]
    ppermute x34, waiting for transfers between devices: 34.4 us -> 40.5 us  [send(): return lax.ppermute(array, BOTH, pairs)]
    ppermute x4 -> x2, waiting for transfers between devices: 2.64 us -> 6.86 us  [halo(): return (lax.ppermute(last, 'row', up), lax.ppermute(first, 'row', down))]
    all_gather x1, waiting for transfers between devices: 0.01 us -> 3.83 us  [per_device(): whole = lax.all_gather(frames, 'col', axis=1, tiled=True)]
    pallas_call x1, Pallas kernels: 58.7 us -> 55 us  [middle(): pl.pallas_call(functools.partial(middle_body, width, rows), grid_spec=plt...]
    ppermute x4, starting transfers between devices: 9.63 us -> 6.25 us  [folded(): return tap_sum + lax.ppermute(tap_sum, 'row', pairs)]
    ppermute x4, waiting for transfers between devices: 7.79 us -> 4.65 us  [folded(): return tap_sum + lax.ppermute(tap_sum, 'row', pairs)]
  transfers between devices with their start and end apart: 44 -> 42, of which waited for: 18 -> 17; matrix products, arithmetic and copies ran while one was open for 10% -> 7% of each run, Pallas kernels for 6% -> 6%
where the time goes in v2:
time: 216 us
  Pallas kernels  68.5 us (32%)
  starting transfers between devices  60.2 us (28%)
  waiting for transfers between devices  56.5 us (26%)
  between operations  14.7 us (7%)
  local copies, waits for them, and re-layouts  9.78 us (5%)
  other arithmetic  6.39 us (3%)
    pallas_call x1, Pallas kernels, middle(): pl.pallas_call(functools.partial(middle_body, width, rows), grid_spec=plt...  55 us
    ppermute x34, starting transfers between devices, send(): return lax.ppermute(array, BOTH, pairs)  47.8 us
    ppermute x34, waiting for transfers between devices, send(): return lax.ppermute(array, BOTH, pairs)  40.5 us
    pallas_call x1, Pallas kernels, weight_parts(): pl.pallas_call(weight_body, grid_spec=pltpu.PrefetchScalarGridSpec(num_sc...  13.5 us
    ppermute x2, waiting for transfers between devices, halo(): return (lax.ppermute(last, 'row', up), lax.ppermute(first, 'row', down))  6.86 us
    ppermute x4, starting transfers between devices, folded(): return tap_sum + lax.ppermute(tap_sum, 'row', pairs)  6.25 us
    ppermute x2, starting transfers between devices, halo(): return (lax.ppermute(last, 'row', up), lax.ppermute(first, 'row', down))  6.02 us
    unnamed x34, local copies, waits for them, and re-layouts  5.42 us
  transfers between devices with their start and end apart: 42, of which 17 were waited for; matrix products, arithmetic and copies ran while one was open for 7% of the time, Pallas kernels for 6%

profile of v2, /device:TPU:42, one launch (start us, length us, event | category | flops | bytes accessed | tf_op | source)
XLA Modules:
  0.0 216.0 jit_solution(16495840147666944399)
XLA Ops:
  7.2 0.7 all-gather.2.cloned.1.call-update
  8.0 1.6 collective-permute-start
  9.6 0.5 collective-permute-start.1
  10.1 1.9 collective-permute-start.4
  12.1 4.2 %collective-permute-done = bf16[256,512]{1,0:T(8,128)(2,1)S(1)} collective-permute-done((bf16[256,512]{1,0:T(8,128)(2,1)}, bf16[256,512]{1,0:T(8,128)(2,1)S(1)}, u32[]{:S(2)}, u32[]{:S(2)}) %collective-permute-start) | collective-permute-done | bytes 262176 | tf_op jit(solution)/shard_map/ppermute | solution.py:50
  16.3 1.6 collective-permute-start.2
  18.0 0.5 collective-permute-start.3
  18.5 2.0 collective-permute-start.6
  20.7 0.7 collective-permute-done.2
  21.3 1.7 collective-permute-done.3
  23.0 0.5 collective-permute-done.6
  23.5 2.0 collective-permute-done.7
  25.5 1.0 constant_dynamic-update-slice_fusion.9
  26.6 1.6 collective-permute-start.12
  28.3 1.4 collective-permute-start.13
  29.7 1.0 constant_dynamic-update-slice_fusion.4
  30.8 1.7 collective-permute-start.8
  32.9 0.8 fusion.21
  33.7 16.7 %collective-permute-done.12.refs_6_ = bf16[4,256,512]{2,1,0:T(8,128)(2,1)S(1)} collective-permute-done((bf16[4,256,512]{2,1,0:T(8,128)(2,1)S(1)}, bf16[4,256,512]{2,1,0:T(8,128)(2,1)S(1)}, u32[]{:S(2)}, u32[]{:S(2)}) %collective-permute-start.12) | collective-permute-done | bytes 1048608 | tf_op jit(solution)/shard_map/ppermute | solution.py:50
  50.4 0.7 collective-permute-start.14
  51.1 2.5 %collective-permute-start.15 = (bf16[2,256,512]{2,1,0:T(8,128)(2,1)S(1)}, bf16[2,256,512]{2,1,0:T(8,128)(2,1)}, u32[]{:S(2)}, u32[]{:S(2)}) collective-permute-start(bf16[2,256,512]{2,1,0:T(8,128)(2,1)S(1)} %slice.155), channel_id=1, source_target_pairs={{0,24},{1,25},{2,26},{3,27},{4,28},{5,29},{6,30},{7,31},{8,0},{9,1... | collective-permute-start | bytes 1572872 | tf_op jit(solution)/shard_map/ppermute | solution.py:50
  53.6 1.7 collective-permute-start.10
  55.4 0.9 copy-done.5
  56.7 3.8 %all-gather.2.cloned.1.call-done.refs_11_.a.b.c.d = bf16[1024,4096]{1,0:T(8,128)(2,1)} async-done(((bf16[1024,512]{1,0:T(8,128)(2,1)}), bf16[1024,4096]{1,0:T(8,128)(2,1)}) %all-gather.2.cloned.1.call-update) | async-done | bytes 8388624 | tf_op jit(solution)/shard_map/all_gather | solution.py:323
  60.5 1.1 fusion.20
  61.6 3.4 %collective-permute-start.16 = (bf16[32,4608]{1,0:T(8,128)(2,1)S(1)}, bf16[32,4608]{1,0:T(8,128)(2,1)}, u32[]{:S(2)}, u32[]{:S(2)}) collective-permute-start(bf16[32,4608]{1,0:T(8,128)(2,1)S(1)} %pad_maximum_fusion), channel_id=1, source_target_pairs={{0,8},{8,16},{16,24},{24,32},{32,40},{40,48},{48,56},{56,64},{64,7... | collective-permute-start | bytes 884744 | tf_op jit(solution)/shard_map/ppermute | solution.py:59
  65.1 2.6 %collective-permute-start.17 = (bf16[32,4608]{1,0:T(8,128)(2,1)S(1)}, bf16[32,4608]{1,0:T(8,128)(2,1)S(1)}, u32[]{:S(2)}, u32[]{:S(2)}) collective-permute-start(bf16[32,4608]{1,0:T(8,128)(2,1)S(1)} %pad_maximum_fusion.1), channel_id=1, source_target_pairs={{8,0},{16,8},{24,16},{32,24},{40,32},{48,40},{56,48},{64,56},{72,6... | collective-permute-start | bytes 884744 | tf_op jit(solution)/shard_map/ppermute | solution.py:59
  67.8 0.6 pad_add_fusion.place
  68.4 0.6 pad_convert_fusion.refs_14_
  69.0 3.8 %collective-permute-done.16.refs_10_ = bf16[32,4608]{1,0:T(8,128)(2,1)} collective-permute-done((bf16[32,4608]{1,0:T(8,128)(2,1)S(1)}, bf16[32,4608]{1,0:T(8,128)(2,1)}, u32[]{:S(2)}, u32[]{:S(2)}) %collective-permute-start.16) | collective-permute-done | bytes 294944 | tf_op jit(solution)/shard_map/ppermute | solution.py:59
  72.8 3.1 %collective-permute-done.17.refs_12_ = bf16[32,4608]{1,0:T(8,128)(2,1)S(1)} collective-permute-done((bf16[32,4608]{1,0:T(8,128)(2,1)S(1)}, bf16[32,4608]{1,0:T(8,128)(2,1)S(1)}, u32[]{:S(2)}, u32[]{:S(2)}) %collective-permute-start.17) | collective-permute-done | bytes 294944 | tf_op jit(solution)/shard_map/ppermute | solution.py:59
  75.9 0.7 copy-done.11
  76.6 55.0 %shard_map.92 = (bf16[1024,512]{1,0:T(8,128)(2,1)}, bf16[2,512,1024]{2,1,0:T(8,128)(2,1)}, bf16[1024,4096]{1,0:T(8,128)(2,1)}, bf16[2,4,512,256]{3,2,1,0:T(8,128)(2,1)}, f32[32,512]{1,0:T(8,128)}) custom-call(s32[3]{0:T(128)} %pad_add_fusion.place, bf16[4,256,512]{2,1,0:T(8,128)(2,1)} %bitcast.101, bf16[4,256,512]{2,1,0:T(8,128)(2,1)} %copy-done.4, ...), custom_call_target="tpu_custom_call" | custom-call | flops 40000000000 | bytes 41943040 | tf_op jit(solution)/shard_map/pallas_call | solution.py:235
  132.3 0.6 concatenate.43.order
  133.0 0.7 collective-permute-start.18
  133.7 1.1 slice_bitcast_fusion
  134.8 1.5 collective-permute-start.21
  136.3 3.8 %collective-permute-start.22 = (bf16[2,512,256]{2,1,0:T(8,128)(2,1)}, bf16[2,512,256]{2,1,0:T(8,128)(2,1)S(1)}, u32[]{:S(2)}, u32[]{:S(2)}) collective-permute-start(bf16[2,512,256]{2,1,0:T(8,128)(2,1)} %get-tuple-element.100), channel_id=1, source_target_pairs={{0,8},{1,25},{2,10},{3,27},{4,12},{5,29},{6,14},{7,31},{8,16},{9,1... | collective-permute-start | bytes 1572872 | tf_op jit(solution)/shard_map/ppermute | solution.py:50
  140.4 13.5 %shard_map.93 = bf16[6,4,512,256]{3,2,1,0:T(8,128)(2,1)} custom-call(s32[6,5]{1,0:T(8,128)} %concatenate.43.order, bf16[2,512,1024]{2,1,0:T(8,128)(2,1)} %get-tuple-element.55.grad, bf16[1024,4096]{1,0:T(8,128)(2,1)} %all-gather.2.cloned.1.call-done.refs_11_.a.b.c.d, bf16[1024,4096]{1,0:T(8,128)(2,1)} %all-gather.2.cloned.1.call-done.refs_11_.a.b.c.d, ...), custom_call_target="tpu_custom_call" | custom-call | flops 6442450944 | bytes 25165824 | tf_op jit(solution)/shard_map/pallas_call | solution.py:284
  153.9 1.6 fusion.7
  155.5 2.1 collective-permute-start.26
  157.9 1.5 fusion.6
  159.4 1.9 collective-permute-start.23
  161.3 3.6 %collective-permute-start.25 = (f32[32,512]{1,0:T(8,128)S(1)}, f32[32,512]{1,0:T(8,128)S(1)}, u32[]{:S(2)}, u32[]{:S(2)}) collective-permute-start(f32[32,512]{1,0:T(8,128)S(1)} %add.221), channel_id=1, source_target_pairs={{0,16},{8,24},{16,0},{24,8},{32,48},{40,56},{48,32},{56,40},{64,80... | collective-permute-start | bytes 196616 | tf_op jit(solution)/shard_map/ppermute | solution.py:353
  164.9 3.0 %collective-permute-done.25 = f32[32,512]{1,0:T(8,128)S(1)} collective-permute-done((f32[32,512]{1,0:T(8,128)S(1)}, f32[32,512]{1,0:T(8,128)S(1)}, u32[]{:S(2)}, u32[]{:S(2)}) %collective-permute-start.25) | collective-permute-done | bytes 65568 | tf_op jit(solution)/shard_map/ppermute | solution.py:353
  168.2 1.9 collective-permute-start.31
  170.2 2.3 %collective-permute-start.32 = (bf16[2,512,256]{2,1,0:T(8,128)(2,1)S(1)}, bf16[2,512,256]{2,1,0:T(8,128)(2,1)S(1)}, u32[]{:S(2)}, u32[]{:S(2)}) collective-permute-start(bf16[2,512,256]{2,1,0:T(8,128)(2,1)S(1)} %get-tuple-element.94), channel_id=1, source_target_pairs={{0,8},{1,25},{2,10},{3,27},{4,12},{5,29},{6,14},{7,31},{8,16},{9,1... | collective-permute-start | bytes 1572872 | tf_op jit(solution)/shard_map/ppermute | solution.py:50
  172.5 1.6 collective-permute-done.24
  174.4 0.7 collective-permute-start.30
  175.1 2.2 %collective-permute-start.28 = (bf16[2,512,256]{2,1,0:T(8,128)(2,1)S(1)}, bf16[2,512,256]{2,1,0:T(8,128)(2,1)S(1)}, u32[]{:S(2)}, u32[]{:S(2)}) collective-permute-start(bf16[2,512,256]{2,1,0:T(8,128)(2,1)S(1)} %get-tuple-element.93), channel_id=1, source_target_pairs={{0,32},{1,97},{2,34},{3,99},{4,36},{5,101},{6,38},{7,103},{8,40},{... | collective-permute-start | bytes 1572872 | tf_op jit(solution)/shard_map/ppermute | solution.py:50
  177.5 1.6 collective-permute-done.30
  179.1 1.7 collective-permute-done.32
  181.1 1.2 collective-permute-start.39
  182.3 1.8 collective-permute-start.36
  184.1 0.8 collective-permute-start.37
  184.9 3.8 %collective-permute-done.28 = bf16[2,512,256]{2,1,0:T(8,128)(2,1)S(1)} collective-permute-done((bf16[2,512,256]{2,1,0:T(8,128)(2,1)S(1)}, bf16[2,512,256]{2,1,0:T(8,128)(2,1)S(1)}, u32[]{:S(2)}, u32[]{:S(2)}) %collective-permute-start.28) | collective-permute-done | bytes 524320 | tf_op jit(solution)/shard_map/ppermute | solution.py:50
  189.1 7.6 %collective-permute-start.38 = (bf16[512,256]{1,0:T(8,128)(2,1)S(1)}, bf16[512,256]{1,0:T(8,128)(2,1)S(1)}, u32[]{:S(2)}, u32[]{:S(2)}) collective-permute-start(bf16[512,256]{1,0:T(8,128)(2,1)S(1)} %slice_bitcast_fusion.4), channel_id=1, source_target_pairs={{0,32},{1,97},{2,34},{3,99},{4,36},{5,101},{6,38},{7,103},{8,40},{... | collective-permute-start | bytes 786440 | tf_op jit(solution)/shard_map/ppermute | solution.py:50
  196.9 2.1 collective-permute-start.35
  199.0 0.6 slice_add_fusion
  199.6 0.9 collective-permute-done.38
  200.7 0.8 copy.11
  201.5 4.4 %collective-permute-done.33 = bf16[512,256]{1,0:T(8,128)(2,1)S(1)} collective-permute-done((bf16[512,256]{1,0:T(8,128)(2,1)S(1)}, bf16[512,256]{1,0:T(8,128)(2,1)S(1)}, u32[]{:S(2)}, u32[]{:S(2)}) %collective-permute-start.33) | collective-permute-done | bytes 262176 | tf_op jit(solution)/shard_map/ppermute | solution.py:50
  205.9 2.2 %collective-permute-done.35 = bf16[512,256]{1,0:T(8,128)(2,1)S(1)} collective-permute-done((bf16[512,256]{1,0:T(8,128)(2,1)S(1)}, bf16[512,256]{1,0:T(8,128)(2,1)S(1)}, u32[]{:S(2)}, u32[]{:S(2)}) %collective-permute-start.35) | collective-permute-done | bytes 262176 | tf_op jit(solution)/shard_map/ppermute | solution.py:50
  208.3 0.8 copy.10
  (98 shorter events, 4.6 us)
Async XLA Ops:
  7.2 61.2 %copy-start.9 = (bf16[31,512]{1,0:T(8,128)(2,1)S(1)}, bf16[31,512]{1,0:T(8,128)(2,1)}, u32[]{:S(2)}) copy-start(bf16[31,512]{1,0:T(8,128)(2,1)} %param.8) | copy-start | bytes 95236
  7.2 53.4 %all-gather.2.cloned.1.call-start = ((), (), s32[]{:S(2)}) async-start(), calls=%async_computation.1 | async-start | bytes 9437184 | tf_op jit(solution)/shard_map/all_gather | solution.py:323
  7.9 201.2 %reduce-scatter.2.cloned.1.call-start = ((), (), s32[]{:S(2)}) async-start(), calls=%async_computation.2 | async-start | bytes 9437184 | tf_op jit(solution)/shard_map/reduce_scatter | solution.py:349
  8.0 8.3 %collective-permute-start = (bf16[256,512]{1,0:T(8,128)(2,1)}, bf16[256,512]{1,0:T(8,128)(2,1)S(1)}, u32[]{:S(2)}, u32[]{:S(2)}) collective-permute-start(bf16[256,512]{1,0:T(8,128)(2,1)} %param.6), channel_id=1, source_target_pairs={{0,8},{1,9},{2,10},{3,11},{4,12},{5,13},{6,14},{7,15},{8,16},{9,17... | collective-permute-start | bytes 786440 | tf_op jit(solution)/shard_map/ppermute | solution.py:50
  9.6 8.3 %collective-permute-start.1 = (bf16[256,512]{1,0:T(8,128)(2,1)}, bf16[256,512]{1,0:T(8,128)(2,1)S(1)}, u32[]{:S(2)}, u32[]{:S(2)}) collective-permute-start(bf16[256,512]{1,0:T(8,128)(2,1)} %param.6), channel_id=1, source_target_pairs={{0,24},{1,25},{2,26},{3,27},{4,28},{5,29},{6,30},{7,31},{8,0},{9,1... | collective-permute-start | bytes 786440 | tf_op jit(solution)/shard_map/ppermute | solution.py:50
  10.1 8.4 %collective-permute-start.4 = (bf16[256,512]{1,0:T(8,128)(2,1)}, bf16[256,512]{1,0:T(8,128)(2,1)S(1)}, u32[]{:S(2)}, u32[]{:S(2)}) collective-permute-start(bf16[256,512]{1,0:T(8,128)(2,1)} %param.7), channel_id=1, source_target_pairs={{0,32},{1,33},{2,34},{3,35},{4,36},{5,37},{6,38},{7,39},{8,40},{9,... | collective-permute-start | bytes 786440 | tf_op jit(solution)/shard_map/ppermute | solution.py:50
  12.0 8.5 %collective-permute-start.5 = (bf16[256,512]{1,0:T(8,128)(2,1)}, bf16[256,512]{1,0:T(8,128)(2,1)S(1)}, u32[]{:S(2)}, u32[]{:S(2)}) collective-permute-start(bf16[256,512]{1,0:T(8,128)(2,1)} %param.7), channel_id=1, source_target_pairs={{0,96},{1,97},{2,98},{3,99},{4,100},{5,101},{6,102},{7,103},{8,104... | collective-permute-start | bytes 786440 | tf_op jit(solution)/shard_map/ppermute | solution.py:50
  16.3 5.0 %collective-permute-start.2 = (bf16[128,512]{1,0:T(8,128)(2,1)S(1)}, bf16[128,512]{1,0:T(8,128)(2,1)S(1)}, u32[]{:S(2)}, u32[]{:S(2)}) collective-permute-start(bf16[128,512]{1,0:T(8,128)(2,1)S(1)} %slice.148), channel_id=1, source_target_pairs={{0,8},{1,9},{2,10},{3,11},{4,12},{5,13},{6,14},{7,15},{8,16},{9,17... | collective-permute-start | bytes 393224 | tf_op jit(solution)/shard_map/ppermute | solution.py:50
  18.0 5.0 %collective-permute-start.3 = (bf16[128,512]{1,0:T(8,128)(2,1)S(1)}, bf16[128,512]{1,0:T(8,128)(2,1)S(1)}, u32[]{:S(2)}, u32[]{:S(2)}) collective-permute-start(bf16[128,512]{1,0:T(8,128)(2,1)S(1)} %slice.149), channel_id=1, source_target_pairs={{0,24},{1,25},{2,26},{3,27},{4,28},{5,29},{6,30},{7,31},{8,0},{9,1... | collective-permute-start | bytes 393224 | tf_op jit(solution)/shard_map/ppermute | solution.py:50
  18.5 5.0 %collective-permute-start.6 = (bf16[128,512]{1,0:T(8,128)(2,1)S(1)}, bf16[128,512]{1,0:T(8,128)(2,1)S(1)}, u32[]{:S(2)}, u32[]{:S(2)}) collective-permute-start(bf16[128,512]{1,0:T(8,128)(2,1)S(1)} %slice.150), channel_id=1, source_target_pairs={{0,32},{1,33},{2,34},{3,35},{4,36},{5,37},{6,38},{7,39},{8,40},{9,... | collective-permute-start | bytes 393224 | tf_op jit(solution)/shard_map/ppermute | solution.py:50
  20.5 5.0 %collective-permute-start.7 = (bf16[128,512]{1,0:T(8,128)(2,1)S(1)}, bf16[128,512]{1,0:T(8,128)(2,1)S(1)}, u32[]{:S(2)}, u32[]{:S(2)}) collective-permute-start(bf16[128,512]{1,0:T(8,128)(2,1)S(1)} %slice.151), channel_id=1, source_target_pairs={{0,96},{1,97},{2,98},{3,99},{4,100},{5,101},{6,102},{7,103},{8,104... | collective-permute-start | bytes 393224 | tf_op jit(solution)/shard_map/ppermute | solution.py:50
  26.6 28.8 %copy-start.7 = (bf16[1024,512]{1,0:T(8,128)(2,1)}, bf16[1024,512]{1,0:T(8,128)(2,1)S(1)}, u32[]{:S(2)}) copy-start(bf16[1024,512]{1,0:T(8,128)(2,1)S(1)} %constant_dynamic-update-slice_fusion.5) | copy-start | bytes 3145732
  26.6 23.8 %collective-permute-start.12 = (bf16[4,256,512]{2,1,0:T(8,128)(2,1)S(1)}, bf16[4,256,512]{2,1,0:T(8,128)(2,1)S(1)}, u32[]{:S(2)}, u32[]{:S(2)}) collective-permute-start(bf16[4,256,512]{2,1,0:T(8,128)(2,1)S(1)} %bitcast.96), channel_id=1, source_target_pairs={{0,8},{1,9},{2,10},{3,11},{4,12},{5,13},{6,14},{7,15},{8,16},{9,17... | collective-permute-start | bytes 3145736 | tf_op jit(solution)/shard_map/ppermute | solution.py:50
  28.3 22.8 %collective-permute-start.13 = (bf16[4,256,512]{2,1,0:T(8,128)(2,1)S(1)}, bf16[4,256,512]{2,1,0:T(8,128)(2,1)S(1)}, u32[]{:S(2)}, u32[]{:S(2)}) collective-permute-start(bf16[4,256,512]{2,1,0:T(8,128)(2,1)S(1)} %bitcast.97), channel_id=1, source_target_pairs={{0,24},{1,25},{2,26},{3,27},{4,28},{5,29},{6,30},{7,31},{8,0},{9,1... | collective-permute-start | bytes 3145736 | tf_op jit(solution)/shard_map/ppermute | solution.py:50
  30.8 24.6 %copy-start.8 = (bf16[1024,512]{1,0:T(8,128)(2,1)}, bf16[1024,512]{1,0:T(8,128)(2,1)S(1)}, u32[]{:S(2)}) copy-start(bf16[1024,512]{1,0:T(8,128)(2,1)S(1)} %constant_dynamic-update-slice_fusion) | copy-start | bytes 3145732
  30.8 22.8 %collective-permute-start.8 = (bf16[4,256,512]{2,1,0:T(8,128)(2,1)S(1)}, bf16[4,256,512]{2,1,0:T(8,128)(2,1)S(1)}, u32[]{:S(2)}, u32[]{:S(2)}) collective-permute-start(bf16[4,256,512]{2,1,0:T(8,128)(2,1)S(1)} %bitcast.99), channel_id=1, source_target_pairs={{0,32},{1,33},{2,34},{3,35},{4,36},{5,37},{6,38},{7,39},{8,40},{9,... | collective-permute-start | bytes 3145736 | tf_op jit(solution)/shard_map/ppermute | solution.py:50
  32.5 22.9 %collective-permute-start.9 = (bf16[4,256,512]{2,1,0:T(8,128)(2,1)S(1)}, bf16[4,256,512]{2,1,0:T(8,128)(2,1)S(1)}, u32[]{:S(2)}, u32[]{:S(2)}) collective-permute-start(bf16[4,256,512]{2,1,0:T(8,128)(2,1)S(1)} %bitcast.100), channel_id=1, source_target_pairs={{0,96},{1,97},{2,98},{3,99},{4,100},{5,101},{6,102},{7,103},{8,104... | collective-permute-start | bytes 3145736 | tf_op jit(solution)/shard_map/ppermute | solution.py:50
  50.4 5.0 %copy-start.2 = (bf16[4,256,512]{2,1,0:T(8,128)(2,1)}, bf16[4,256,512]{2,1,0:T(8,128)(2,1)S(1)}, u32[]{:S(2)}) copy-start(bf16[4,256,512]{2,1,0:T(8,128)(2,1)S(1)} %collective-permute-done.12.refs_6_) | copy-start | bytes 3145732
  50.4 14.7 %collective-permute-start.14 = (bf16[2,256,512]{2,1,0:T(8,128)(2,1)S(1)}, bf16[2,256,512]{2,1,0:T(8,128)(2,1)S(1)}, u32[]{:S(2)}, u32[]{:S(2)}) collective-permute-start(bf16[2,256,512]{2,1,0:T(8,128)(2,1)S(1)} %slice.154), channel_id=1, source_target_pairs={{0,8},{1,9},{2,10},{3,11},{4,12},{5,13},{6,14},{7,15},{8,16},{9,17... | collective-permute-start | bytes 1572872 | tf_op jit(solution)/shard_map/ppermute | solution.py:50
  51.1 2.5 %copy-start.3 = (bf16[4,256,512]{2,1,0:T(8,128)(2,1)}, bf16[4,256,512]{2,1,0:T(8,128)(2,1)S(1)}, u32[]{:S(2)}) copy-start(bf16[4,256,512]{2,1,0:T(8,128)(2,1)S(1)} %collective-permute-done.13.refs_7_) | copy-start | bytes 3145732
  51.1 17.9 %collective-permute-start.15 = (bf16[2,256,512]{2,1,0:T(8,128)(2,1)S(1)}, bf16[2,256,512]{2,1,0:T(8,128)(2,1)}, u32[]{:S(2)}, u32[]{:S(2)}) collective-permute-start(bf16[2,256,512]{2,1,0:T(8,128)(2,1)S(1)} %slice.155), channel_id=1, source_target_pairs={{0,24},{1,25},{2,26},{3,27},{4,28},{5,29},{6,30},{7,31},{8,0},{9,1... | collective-permute-start | bytes 1572872 | tf_op jit(solution)/shard_map/ppermute | solution.py:50
  53.6 1.8 copy-start.4
  53.6 15.4 %collective-permute-start.10 = (bf16[2,256,512]{2,1,0:T(8,128)(2,1)S(1)}, bf16[2,256,512]{2,1,0:T(8,128)(2,1)}, u32[]{:S(2)}, u32[]{:S(2)}) collective-permute-start(bf16[2,256,512]{2,1,0:T(8,128)(2,1)S(1)} %slice.152), channel_id=1, source_target_pairs={{0,32},{1,33},{2,34},{3,35},{4,36},{5,37},{6,38},{7,39},{8,40},{9,... | collective-permute-start | bytes 1572872 | tf_op jit(solution)/shard_map/ppermute | solution.py:50
  55.3 1.0 copy-start.5
  56.3 12.7 %collective-permute-start.11 = (bf16[2,256,512]{2,1,0:T(8,128)(2,1)S(1)}, bf16[2,256,512]{2,1,0:T(8,128)(2,1)}, u32[]{:S(2)}, u32[]{:S(2)}) collective-permute-start(bf16[2,256,512]{2,1,0:T(8,128)(2,1)S(1)} %slice.153), channel_id=1, source_target_pairs={{0,96},{1,97},{2,98},{3,99},{4,100},{5,101},{6,102},{7,103},{8,104... | collective-permute-start | bytes 1572872 | tf_op jit(solution)/shard_map/ppermute | solution.py:50
  61.6 11.2 %collective-permute-start.16 = (bf16[32,4608]{1,0:T(8,128)(2,1)S(1)}, bf16[32,4608]{1,0:T(8,128)(2,1)}, u32[]{:S(2)}, u32[]{:S(2)}) collective-permute-start(bf16[32,4608]{1,0:T(8,128)(2,1)S(1)} %pad_maximum_fusion), channel_id=1, source_target_pairs={{0,8},{8,16},{16,24},{24,32},{32,40},{40,48},{48,56},{56,64},{64,7... | collective-permute-start | bytes 884744 | tf_op jit(solution)/shard_map/ppermute | solution.py:59
  65.1 10.8 %copy-start.10 = (bf16[2,256,512]{2,1,0:T(8,128)(2,1)}, bf16[2,256,512]{2,1,0:T(8,128)(2,1)S(1)}, u32[]{:S(2)}) copy-start(bf16[2,256,512]{2,1,0:T(8,128)(2,1)S(1)} %collective-permute-done.14.refs_8_) | copy-start | bytes 1572868
  65.1 10.8 %collective-permute-start.17 = (bf16[32,4608]{1,0:T(8,128)(2,1)S(1)}, bf16[32,4608]{1,0:T(8,128)(2,1)S(1)}, u32[]{:S(2)}, u32[]{:S(2)}) collective-permute-start(bf16[32,4608]{1,0:T(8,128)(2,1)S(1)} %pad_maximum_fusion.1), channel_id=1, source_target_pairs={{8,0},{16,8},{24,16},{32,24},{40,32},{48,40},{56,48},{64,56},{72,6... | collective-permute-start | bytes 884744 | tf_op jit(solution)/shard_map/ppermute | solution.py:59
  75.9 0.7 copy-start.11
  131.6 1.3 copy-start.6
  131.6 2.1 copy-start.1
  133.0 20.9 %collective-permute-start.18 = (f32[32,512]{1,0:T(8,128)S(1)}, f32[32,512]{1,0:T(8,128)S(1)}, u32[]{:S(2)}, u32[]{:S(2)}) collective-permute-start(f32[32,512]{1,0:T(8,128)S(1)} %copy-done.6), channel_id=1, source_target_pairs={{0,8},{8,0},{16,24},{24,16},{32,40},{40,32},{48,56},{56,48},{64,72... | collective-permute-start | bytes 196616 | tf_op jit(solution)/shard_map/ppermute | solution.py:353
  134.8 19.1 %collective-permute-start.21 = (bf16[2,512,256]{2,1,0:T(8,128)(2,1)}, bf16[2,512,256]{2,1,0:T(8,128)(2,1)S(1)}, u32[]{:S(2)}, u32[]{:S(2)}) collective-permute-start(bf16[2,512,256]{2,1,0:T(8,128)(2,1)} %get-tuple-element.101), channel_id=1, source_target_pairs={{0,32},{1,97},{2,34},{3,99},{4,36},{5,101},{6,38},{7,103},{8,40},{... | collective-permute-start | bytes 1572872 | tf_op jit(solution)/shard_map/ppermute | solution.py:50
  136.3 17.6 %collective-permute-start.22 = (bf16[2,512,256]{2,1,0:T(8,128)(2,1)}, bf16[2,512,256]{2,1,0:T(8,128)(2,1)S(1)}, u32[]{:S(2)}, u32[]{:S(2)}) collective-permute-start(bf16[2,512,256]{2,1,0:T(8,128)(2,1)} %get-tuple-element.100), channel_id=1, source_target_pairs={{0,8},{1,25},{2,10},{3,27},{4,12},{5,29},{6,14},{7,31},{8,16},{9,1... | collective-permute-start | bytes 1572872 | tf_op jit(solution)/shard_map/ppermute | solution.py:50
  140.1 17.8 %collective-permute-start.19 = (bf16[2,512,256]{2,1,0:T(8,128)(2,1)S(1)}, bf16[2,512,256]{2,1,0:T(8,128)(2,1)S(1)}, u32[]{:S(2)}, u32[]{:S(2)}) collective-permute-start(bf16[2,512,256]{2,1,0:T(8,128)(2,1)S(1)} %get-tuple-element.103), channel_id=1, source_target_pairs={{0,32},{1,97},{2,34},{3,99},{4,36},{5,101},{6,38},{7,103},{8,40},{... | collective-permute-start | bytes 1572872 | tf_op jit(solution)/shard_map/ppermute | solution.py:50
  140.1 17.8 %collective-permute-start.20 = (bf16[2,512,256]{2,1,0:T(8,128)(2,1)S(1)}, bf16[2,512,256]{2,1,0:T(8,128)(2,1)S(1)}, u32[]{:S(2)}, u32[]{:S(2)}) collective-permute-start(bf16[2,512,256]{2,1,0:T(8,128)(2,1)S(1)} %get-tuple-element.102), channel_id=1, source_target_pairs={{0,8},{1,25},{2,10},{3,27},{4,12},{5,29},{6,14},{7,31},{8,16},{9,1... | collective-permute-start | bytes 1572872 | tf_op jit(solution)/shard_map/ppermute | solution.py:50
  153.9 14.1 %copy-start = (bf16[6,4,512,256]{3,2,1,0:T(8,128)(2,1)S(1)}, bf16[6,4,512,256]{3,2,1,0:T(8,128)(2,1)}, u32[]{:S(2)}) copy-start(bf16[6,4,512,256]{3,2,1,0:T(8,128)(2,1)} %shard_map.93) | copy-start | bytes 18874372
  155.5 12.4 %collective-permute-start.26 = (bf16[2,512,256]{2,1,0:T(8,128)(2,1)S(1)}, bf16[2,512,256]{2,1,0:T(8,128)(2,1)S(1)}, u32[]{:S(2)}, u32[]{:S(2)}) collective-permute-start(bf16[2,512,256]{2,1,0:T(8,128)(2,1)S(1)} %get-tuple-element.99), channel_id=1, source_target_pairs={{0,32},{1,97},{2,34},{3,99},{4,36},{5,101},{6,38},{7,103},{8,40},{... | collective-permute-start | bytes 1572872 | tf_op jit(solution)/shard_map/ppermute | solution.py:50
  157.7 10.3 %collective-permute-start.27 = (bf16[2,512,256]{2,1,0:T(8,128)(2,1)S(1)}, bf16[2,512,256]{2,1,0:T(8,128)(2,1)S(1)}, u32[]{:S(2)}, u32[]{:S(2)}) collective-permute-start(bf16[2,512,256]{2,1,0:T(8,128)(2,1)S(1)} %get-tuple-element.98), channel_id=1, source_target_pairs={{0,8},{1,25},{2,10},{3,27},{4,12},{5,29},{6,14},{7,31},{8,16},{9,1... | collective-permute-start | bytes 1572872 | tf_op jit(solution)/shard_map/ppermute | solution.py:50
  159.4 13.1 %collective-permute-start.23 = (bf16[2,512,256]{2,1,0:T(8,128)(2,1)S(1)}, bf16[2,512,256]{2,1,0:T(8,128)(2,1)S(1)}, u32[]{:S(2)}, u32[]{:S(2)}) collective-permute-start(bf16[2,512,256]{2,1,0:T(8,128)(2,1)S(1)} %get-tuple-element.97), channel_id=1, source_target_pairs={{0,32},{1,97},{2,34},{3,99},{4,36},{5,101},{6,38},{7,103},{8,40},{... | collective-permute-start | bytes 1572872 | tf_op jit(solution)/shard_map/ppermute | solution.py:50
  161.3 6.6 %collective-permute-start.25 = (f32[32,512]{1,0:T(8,128)S(1)}, f32[32,512]{1,0:T(8,128)S(1)}, u32[]{:S(2)}, u32[]{:S(2)}) collective-permute-start(f32[32,512]{1,0:T(8,128)S(1)} %add.221), channel_id=1, source_target_pairs={{0,16},{8,24},{16,0},{24,8},{32,48},{40,56},{48,32},{56,40},{64,80... | collective-permute-start | bytes 196616 | tf_op jit(solution)/shard_map/ppermute | solution.py:353
  164.9 9.2 %collective-permute-start.24 = (bf16[2,512,256]{2,1,0:T(8,128)(2,1)S(1)}, bf16[2,512,256]{2,1,0:T(8,128)(2,1)S(1)}, u32[]{:S(2)}, u32[]{:S(2)}) collective-permute-start(bf16[2,512,256]{2,1,0:T(8,128)(2,1)S(1)} %get-tuple-element.96), channel_id=1, source_target_pairs={{0,8},{1,25},{2,10},{3,27},{4,12},{5,29},{6,14},{7,31},{8,16},{9,1... | collective-permute-start | bytes 1572872 | tf_op jit(solution)/shard_map/ppermute | solution.py:50
  168.2 10.9 %collective-permute-start.31 = (bf16[2,512,256]{2,1,0:T(8,128)(2,1)S(1)}, bf16[2,512,256]{2,1,0:T(8,128)(2,1)S(1)}, u32[]{:S(2)}, u32[]{:S(2)}) collective-permute-start(bf16[2,512,256]{2,1,0:T(8,128)(2,1)S(1)} %get-tuple-element.95), channel_id=1, source_target_pairs={{0,32},{1,97},{2,34},{3,99},{4,36},{5,101},{6,38},{7,103},{8,40},{... | collective-permute-start | bytes 1572872 | tf_op jit(solution)/shard_map/ppermute | solution.py:50
  170.2 10.6 %collective-permute-start.32 = (bf16[2,512,256]{2,1,0:T(8,128)(2,1)S(1)}, bf16[2,512,256]{2,1,0:T(8,128)(2,1)S(1)}, u32[]{:S(2)}, u32[]{:S(2)}) collective-permute-start(bf16[2,512,256]{2,1,0:T(8,128)(2,1)S(1)} %get-tuple-element.94), channel_id=1, source_target_pairs={{0,8},{1,25},{2,10},{3,27},{4,12},{5,29},{6,14},{7,31},{8,16},{9,1... | collective-permute-start | bytes 1572872 | tf_op jit(solution)/shard_map/ppermute | solution.py:50
  174.4 4.7 %collective-permute-start.30 = (f32[32,512]{1,0:T(8,128)S(1)}, f32[32,512]{1,0:T(8,128)S(1)}, u32[]{:S(2)}, u32[]{:S(2)}) collective-permute-start(f32[32,512]{1,0:T(8,128)S(1)} %add.226), channel_id=1, source_target_pairs={{0,32},{8,40},{16,48},{24,56},{32,0},{40,8},{48,16},{56,24},{64,96... | collective-permute-start | bytes 196616 | tf_op jit(solution)/shard_map/ppermute | solution.py:353
  175.1 13.7 %collective-permute-start.28 = (bf16[2,512,256]{2,1,0:T(8,128)(2,1)S(1)}, bf16[2,512,256]{2,1,0:T(8,128)(2,1)S(1)}, u32[]{:S(2)}, u32[]{:S(2)}) collective-permute-start(bf16[2,512,256]{2,1,0:T(8,128)(2,1)S(1)} %get-tuple-element.93), channel_id=1, source_target_pairs={{0,32},{1,97},{2,34},{3,99},{4,36},{5,101},{6,38},{7,103},{8,40},{... | collective-permute-start | bytes 1572872 | tf_op jit(solution)/shard_map/ppermute | solution.py:50
  177.3 11.5 %collective-permute-start.29 = (bf16[2,512,256]{2,1,0:T(8,128)(2,1)S(1)}, bf16[2,512,256]{2,1,0:T(8,128)(2,1)S(1)}, u32[]{:S(2)}, u32[]{:S(2)}) collective-permute-start(bf16[2,512,256]{2,1,0:T(8,128)(2,1)S(1)} %get-tuple-element.92), channel_id=1, source_target_pairs={{0,8},{1,25},{2,10},{3,27},{4,12},{5,29},{6,14},{7,31},{8,16},{9,1... | collective-permute-start | bytes 1572872 | tf_op jit(solution)/shard_map/ppermute | solution.py:50
  181.1 15.7 %collective-permute-start.39 = (f32[32,512]{1,0:T(8,128)S(1)}, f32[32,512]{1,0:T(8,128)S(1)}, u32[]{:S(2)}, u32[]{:S(2)}) collective-permute-start(f32[32,512]{1,0:T(8,128)S(1)} %add.231), channel_id=1, source_target_pairs={{0,64},{8,72},{16,80},{24,88},{32,96},{40,104},{48,112},{56,120},{... | collective-permute-start | bytes 196616 | tf_op jit(solution)/shard_map/ppermute | solution.py:353
  182.3 14.6 %collective-permute-start.36 = (bf16[512,256]{1,0:T(8,128)(2,1)S(1)}, bf16[512,256]{1,0:T(8,128)(2,1)S(1)}, u32[]{:S(2)}, u32[]{:S(2)}) collective-permute-start(bf16[512,256]{1,0:T(8,128)(2,1)S(1)} %get-tuple-element.106), channel_id=1, source_target_pairs={{0,96},{1,33},{2,98},{3,35},{4,100},{5,37},{6,102},{7,39},{8,104},... | collective-permute-start | bytes 786440 | tf_op jit(solution)/shard_map/ppermute | solution.py:50
  184.1 15.5 %collective-permute-start.37 = (bf16[512,256]{1,0:T(8,128)(2,1)S(1)}, bf16[512,256]{1,0:T(8,128)(2,1)S(1)}, u32[]{:S(2)}, u32[]{:S(2)}) collective-permute-start(bf16[512,256]{1,0:T(8,128)(2,1)S(1)} %get-tuple-element.107), channel_id=1, source_target_pairs={{0,64},{1,65},{2,66},{3,67},{4,68},{5,69},{6,70},{7,71},{8,72},{9,... | collective-permute-start | bytes 786440 | tf_op jit(solution)/shard_map/ppermute | solution.py:50
  189.1 11.5 %collective-permute-start.38 = (bf16[512,256]{1,0:T(8,128)(2,1)S(1)}, bf16[512,256]{1,0:T(8,128)(2,1)S(1)}, u32[]{:S(2)}, u32[]{:S(2)}) collective-permute-start(bf16[512,256]{1,0:T(8,128)(2,1)S(1)} %slice_bitcast_fusion.4), channel_id=1, source_target_pairs={{0,32},{1,97},{2,34},{3,99},{4,36},{5,101},{6,38},{7,103},{8,40},{... | collective-permute-start | bytes 786440 | tf_op jit(solution)/shard_map/ppermute | solution.py:50
  196.7 9.2 %collective-permute-start.33 = (bf16[512,256]{1,0:T(8,128)(2,1)S(1)}, bf16[512,256]{1,0:T(8,128)(2,1)S(1)}, u32[]{:S(2)}, u32[]{:S(2)}) collective-permute-start(bf16[512,256]{1,0:T(8,128)(2,1)S(1)} %get-tuple-element.108), channel_id=1, source_target_pairs={{0,24},{1,9},{2,26},{3,11},{4,28},{5,13},{6,30},{7,15},{8,0},{9,17... | collective-permute-start | bytes 786440 | tf_op jit(solution)/shard_map/ppermute | solution.py:50
  196.8 9.1 %collective-permute-start.34 = (bf16[512,256]{1,0:T(8,128)(2,1)S(1)}, bf16[512,256]{1,0:T(8,128)(2,1)S(1)}, u32[]{:S(2)}, u32[]{:S(2)}) collective-permute-start(bf16[512,256]{1,0:T(8,128)(2,1)S(1)} %get-tuple-element.109), channel_id=1, source_target_pairs={{0,16},{1,17},{2,18},{3,19},{4,20},{5,21},{6,22},{7,23},{8,24},{9,... | collective-permute-start | bytes 786440 | tf_op jit(solution)/shard_map/ppermute | solution.py:50
  196.9 11.3 %collective-permute-start.35 = (bf16[512,256]{1,0:T(8,128)(2,1)S(1)}, bf16[512,256]{1,0:T(8,128)(2,1)S(1)}, u32[]{:S(2)}, u32[]{:S(2)}) collective-permute-start(bf16[512,256]{1,0:T(8,128)(2,1)S(1)} %slice_bitcast_fusion.6), channel_id=1, source_target_pairs={{0,8},{1,25},{2,10},{3,27},{4,12},{5,29},{6,14},{7,31},{8,16},{9,1... | collective-permute-start | bytes 786440 | tf_op jit(solution)/shard_map/ppermute | solution.py:50
Sparse Core Ops, SparseCore 0:
  9.7 50.7 all-gather.1
  131.8 52.8 reduce-scatter.1

commit v3 on v2

--- a/solution.py
+++ b/solution.py
@@ -81,6 +81,7 @@
         (grad_out, gout.at[pl.ds(EDGE, rows), :]),
         (after.at[:, pl.ds(width_in, channels)], gout.at[pl.ds(EDGE + rows, EDGE), :]),
     ]
+    strip_copies = [[] for _ in range(strips)]
     for kind in range(2):
         for far in range(RING):
             for near in range(RING):
@@ -91,17 +92,29 @@
                 a, b = (near, far) if kind else (far, near)
                 row = lax.rem(z + OFFSETS[a] + RING, RING) * RING
                 row = row + lax.rem(y + OFFSETS[b] + RING, RING)
-                copies.append((source, weights.at[row, :, pl.ds(kind * channels, channels)]))
-    copies = [
-        pltpu.make_async_copy(source, target, in_sem.at[n])
-        for n, (source, target) in enumerate(copies)
-    ]
+                for part in range(strips):
+                    start = kind * channels + part * LANES
+                    target = weights.at[row, :, pl.ds(start, LANES)]
+                    strip_copies[part].append((source.at[:, pl.ds(part * LANES, LANES)], target))
+    strip_copies[0] = copies + strip_copies[0]
+    count = 0
+    for part in range(strips):
+        for n, (source, target) in enumerate(strip_copies[part]):
+            strip_copies[part][n] = pltpu.make_async_copy(source, target, in_sem.at[count])
+            count += 1
+
     @pl.when(strip == 0)
     def _():
-        for copy in copies:
-            copy.start()
-        for copy in copies:
-            copy.wait()
+        for copies in strip_copies:
+            for copy in copies:
+                copy.start()
+
+    for part in range(strips):
+
+        @pl.when(strip == part)
+        def _():
+            for copy in strip_copies[part]:
+                copy.wait()
 
     @pl.when(strip < strips)
     def _():
@@ -252,7 +265,7 @@
                 pltpu.VMEM((rows, 2 * channels), BF16),
                 pltpu.VMEM((total, inner), BF16),
                 pltpu.VMEM((RING * RING, depth, 2 * channels), BF16),
-                pltpu.SemaphoreType.DMA((2 * RING * RING + 6,)),
+                pltpu.SemaphoreType.DMA((2 * RING * RING * count + 6,)),
             ],
         ),
         out_shape=[

time: 216 us -> 217 us (level)
  starting transfers between devices: 60.2 us -> 54.8 us
  waiting for transfers between devices: 56.5 us -> 61.8 us
    ppermute x34, starting transfers between devices: 47.8 us -> 42.3 us  [send(): return lax.ppermute(array, BOTH, pairs)]
    ppermute x34, waiting for transfers between devices: 40.5 us -> 46 us  [send(): return lax.ppermute(array, BOTH, pairs)]
where the time goes in v3:
time: 217 us; the launch traced here: 216 us
  Pallas kernels  68.8 us (32%)
  waiting for transfers between devices  61.8 us (28%)
  starting transfers between devices  54.8 us (25%)
  between operations  14.7 us (7%)
  local copies, waits for them, and re-layouts  9.78 us (5%)
  other arithmetic  6.38 us (3%)
    pallas_call x1, Pallas kernels, middle(): pl.pallas_call(functools.partial(middle_body, width, rows), grid_spec=plt...  55.3 us
    ppermute x34, waiting for transfers between devices, send(): return lax.ppermute(array, BOTH, pairs)  46 us
    ppermute x34, starting transfers between devices, send(): return lax.ppermute(array, BOTH, pairs)  42.3 us
    pallas_call x1, Pallas kernels, weight_parts(): pl.pallas_call(weight_body, grid_spec=pltpu.PrefetchScalarGridSpec(num_sc...  13.5 us
    ppermute x2, waiting for transfers between devices, halo(): return (lax.ppermute(last, 'row', up), lax.ppermute(first, 'row', down))  6.86 us
    ppermute x4, starting transfers between devices, folded(): return tap_sum + lax.ppermute(tap_sum, 'row', pairs)  6.47 us
    ppermute x2, starting transfers between devices, halo(): return (lax.ppermute(last, 'row', up), lax.ppermute(first, 'row', down))  6.02 us
    unnamed x34, local copies, waits for them, and re-layouts  5.42 us
  transfers between devices with their start and end apart: 42, of which 17 were waited for; matrix products, arithmetic and copies ran while one was open for 7% of the time, Pallas kernels for 6%

profile of v3, /device:TPU:42, one launch (start us, length us, event | category | flops | bytes accessed | tf_op | source)
XLA Modules:
  0.0 216.3 jit_solution(7819552582901462007)
XLA Ops:
  7.2 0.7 all-gather.2.cloned.1.call-update
  8.0 1.6 collective-permute-start
  9.6 0.5 collective-permute-start.1
  10.1 1.9 collective-permute-start.4
  12.1 4.2 %collective-permute-done = bf16[256,512]{1,0:T(8,128)(2,1)S(1)} collective-permute-done((bf16[256,512]{1,0:T(8,128)(2,1)}, bf16[256,512]{1,0:T(8,128)(2,1)S(1)}, u32[]{:S(2)}, u32[]{:S(2)}) %collective-permute-start) | collective-permute-done | bytes 262176 | tf_op jit(solution)/shard_map/ppermute | solution.py:50
  16.3 1.6 collective-permute-start.2
  18.0 0.5 collective-permute-start.3
  18.5 2.0 collective-permute-start.6
  20.7 0.7 collective-permute-done.2
  21.3 1.7 collective-permute-done.3
  23.0 0.5 collective-permute-done.6
  23.5 2.0 collective-permute-done.7
  25.5 1.0 constant_dynamic-update-slice_fusion.9
  26.6 1.6 collective-permute-start.12
  28.3 1.4 collective-permute-start.13
  29.7 1.0 constant_dynamic-update-slice_fusion.4
  30.8 1.7 collective-permute-start.8
  32.9 0.8 fusion.21
  33.7 16.7 %collective-permute-done.12.refs_6_ = bf16[4,256,512]{2,1,0:T(8,128)(2,1)S(1)} collective-permute-done((bf16[4,256,512]{2,1,0:T(8,128)(2,1)S(1)}, bf16[4,256,512]{2,1,0:T(8,128)(2,1)S(1)}, u32[]{:S(2)}, u32[]{:S(2)}) %collective-permute-start.12) | collective-permute-done | bytes 1048608 | tf_op jit(solution)/shard_map/ppermute | solution.py:50
  50.4 0.7 collective-permute-start.14
  51.1 2.5 %collective-permute-start.15 = (bf16[2,256,512]{2,1,0:T(8,128)(2,1)S(1)}, bf16[2,256,512]{2,1,0:T(8,128)(2,1)}, u32[]{:S(2)}, u32[]{:S(2)}) collective-permute-start(bf16[2,256,512]{2,1,0:T(8,128)(2,1)S(1)} %slice.155), channel_id=1, source_target_pairs={{0,24},{1,25},{2,26},{3,27},{4,28},{5,29},{6,30},{7,31},{8,0},{9,1... | collective-permute-start | bytes 1572872 | tf_op jit(solution)/shard_map/ppermute | solution.py:50
  53.6 1.7 collective-permute-start.10
  55.4 0.9 copy-done.5
  56.7 3.8 %all-gather.2.cloned.1.call-done.refs_11_.a.b.c.d = bf16[1024,4096]{1,0:T(8,128)(2,1)} async-done(((bf16[1024,512]{1,0:T(8,128)(2,1)}), bf16[1024,4096]{1,0:T(8,128)(2,1)}) %all-gather.2.cloned.1.call-update) | async-done | bytes 8388624 | tf_op jit(solution)/shard_map/all_gather | solution.py:336
  60.5 1.1 fusion.20
  61.6 3.4 %collective-permute-start.16 = (bf16[32,4608]{1,0:T(8,128)(2,1)S(1)}, bf16[32,4608]{1,0:T(8,128)(2,1)}, u32[]{:S(2)}, u32[]{:S(2)}) collective-permute-start(bf16[32,4608]{1,0:T(8,128)(2,1)S(1)} %pad_maximum_fusion), channel_id=1, source_target_pairs={{0,8},{8,16},{16,24},{24,32},{32,40},{40,48},{48,56},{56,64},{64,7... | collective-permute-start | bytes 884744 | tf_op jit(solution)/shard_map/ppermute | solution.py:59
  65.1 2.6 %collective-permute-start.17 = (bf16[32,4608]{1,0:T(8,128)(2,1)S(1)}, bf16[32,4608]{1,0:T(8,128)(2,1)S(1)}, u32[]{:S(2)}, u32[]{:S(2)}) collective-permute-start(bf16[32,4608]{1,0:T(8,128)(2,1)S(1)} %pad_maximum_fusion.1), channel_id=1, source_target_pairs={{8,0},{16,8},{24,16},{32,24},{40,32},{48,40},{56,48},{64,56},{72,6... | collective-permute-start | bytes 884744 | tf_op jit(solution)/shard_map/ppermute | solution.py:59
  67.8 0.6 pad_add_fusion.place
  68.4 0.6 pad_convert_fusion.refs_14_
  69.0 3.8 %collective-permute-done.16.refs_10_ = bf16[32,4608]{1,0:T(8,128)(2,1)} collective-permute-done((bf16[32,4608]{1,0:T(8,128)(2,1)S(1)}, bf16[32,4608]{1,0:T(8,128)(2,1)}, u32[]{:S(2)}, u32[]{:S(2)}) %collective-permute-start.16) | collective-permute-done | bytes 294944 | tf_op jit(solution)/shard_map/ppermute | solution.py:59
  72.8 3.1 %collective-permute-done.17.refs_12_ = bf16[32,4608]{1,0:T(8,128)(2,1)S(1)} collective-permute-done((bf16[32,4608]{1,0:T(8,128)(2,1)S(1)}, bf16[32,4608]{1,0:T(8,128)(2,1)S(1)}, u32[]{:S(2)}, u32[]{:S(2)}) %collective-permute-start.17) | collective-permute-done | bytes 294944 | tf_op jit(solution)/shard_map/ppermute | solution.py:59
  75.9 0.7 copy-done.11
  76.6 55.3 %shard_map.92 = (bf16[1024,512]{1,0:T(8,128)(2,1)}, bf16[2,512,1024]{2,1,0:T(8,128)(2,1)}, bf16[1024,4096]{1,0:T(8,128)(2,1)}, bf16[2,4,512,256]{3,2,1,0:T(8,128)(2,1)}, f32[32,512]{1,0:T(8,128)}) custom-call(s32[3]{0:T(128)} %pad_add_fusion.place, bf16[4,256,512]{2,1,0:T(8,128)(2,1)} %bitcast.101, bf16[4,256,512]{2,1,0:T(8,128)(2,1)} %copy-done.4, ...), custom_call_target="tpu_custom_call" | custom-call | flops 40000000000 | bytes 41943040 | tf_op jit(solution)/shard_map/pallas_call | solution.py:248
  132.6 0.6 concatenate.43.order
  133.3 0.7 collective-permute-start.18
  134.0 1.1 slice_bitcast_fusion
  135.1 1.6 collective-permute-start.21
  136.6 3.8 %collective-permute-start.22 = (bf16[2,512,256]{2,1,0:T(8,128)(2,1)}, bf16[2,512,256]{2,1,0:T(8,128)(2,1)S(1)}, u32[]{:S(2)}, u32[]{:S(2)}) collective-permute-start(bf16[2,512,256]{2,1,0:T(8,128)(2,1)} %get-tuple-element.100), channel_id=1, source_target_pairs={{0,8},{1,25},{2,10},{3,27},{4,12},{5,29},{6,14},{7,31},{8,16},{9,1... | collective-permute-start | bytes 1572872 | tf_op jit(solution)/shard_map/ppermute | solution.py:50
  140.7 13.5 %shard_map.93 = bf16[6,4,512,256]{3,2,1,0:T(8,128)(2,1)} custom-call(s32[6,5]{1,0:T(8,128)} %concatenate.43.order, bf16[2,512,1024]{2,1,0:T(8,128)(2,1)} %get-tuple-element.55.grad, bf16[1024,4096]{1,0:T(8,128)(2,1)} %all-gather.2.cloned.1.call-done.refs_11_.a.b.c.d, bf16[1024,4096]{1,0:T(8,128)(2,1)} %all-gather.2.cloned.1.call-done.refs_11_.a.b.c.d, ...), custom_call_target="tpu_custom_call" | custom-call | flops 6442450944 | bytes 25165824 | tf_op jit(solution)/shard_map/pallas_call | solution.py:297
  154.2 1.6 fusion.7
  155.8 2.3 %collective-permute-start.26 = (bf16[2,512,256]{2,1,0:T(8,128)(2,1)S(1)}, bf16[2,512,256]{2,1,0:T(8,128)(2,1)S(1)}, u32[]{:S(2)}, u32[]{:S(2)}) collective-permute-start(bf16[2,512,256]{2,1,0:T(8,128)(2,1)S(1)} %get-tuple-element.99), channel_id=1, source_target_pairs={{0,32},{1,97},{2,34},{3,99},{4,36},{5,101},{6,38},{7,103},{8,40},{... | collective-permute-start | bytes 1572872 | tf_op jit(solution)/shard_map/ppermute | solution.py:50
  158.2 1.5 fusion.6
  159.7 1.9 collective-permute-start.23
  161.6 3.6 %collective-permute-start.25 = (f32[32,512]{1,0:T(8,128)S(1)}, f32[32,512]{1,0:T(8,128)S(1)}, u32[]{:S(2)}, u32[]{:S(2)}) collective-permute-start(f32[32,512]{1,0:T(8,128)S(1)} %add.221), channel_id=1, source_target_pairs={{0,16},{8,24},{16,0},{24,8},{32,48},{40,56},{48,32},{56,40},{64,80... | collective-permute-start | bytes 196616 | tf_op jit(solution)/shard_map/ppermute | solution.py:366
  165.2 3.0 %collective-permute-done.25 = f32[32,512]{1,0:T(8,128)S(1)} collective-permute-done((f32[32,512]{1,0:T(8,128)S(1)}, f32[32,512]{1,0:T(8,128)S(1)}, u32[]{:S(2)}, u32[]{:S(2)}) %collective-permute-start.25) | collective-permute-done | bytes 65568 | tf_op jit(solution)/shard_map/ppermute | solution.py:366
  168.5 1.7 collective-permute-start.31
  170.3 2.3 %collective-permute-start.32 = (bf16[2,512,256]{2,1,0:T(8,128)(2,1)S(1)}, bf16[2,512,256]{2,1,0:T(8,128)(2,1)S(1)}, u32[]{:S(2)}, u32[]{:S(2)}) collective-permute-start(bf16[2,512,256]{2,1,0:T(8,128)(2,1)S(1)} %get-tuple-element.94), channel_id=1, source_target_pairs={{0,8},{1,25},{2,10},{3,27},{4,12},{5,29},{6,14},{7,31},{8,16},{9,1... | collective-permute-start | bytes 1572872 | tf_op jit(solution)/shard_map/ppermute | solution.py:50
  172.6 1.8 collective-permute-done.24
  174.7 0.7 collective-permute-start.30
  175.3 2.2 %collective-permute-start.28 = (bf16[2,512,256]{2,1,0:T(8,128)(2,1)S(1)}, bf16[2,512,256]{2,1,0:T(8,128)(2,1)S(1)}, u32[]{:S(2)}, u32[]{:S(2)}) collective-permute-start(bf16[2,512,256]{2,1,0:T(8,128)(2,1)S(1)} %get-tuple-element.93), channel_id=1, source_target_pairs={{0,32},{1,97},{2,34},{3,99},{4,36},{5,101},{6,38},{7,103},{8,40},{... | collective-permute-start | bytes 1572872 | tf_op jit(solution)/shard_map/ppermute | solution.py:50
  177.8 1.4 collective-permute-done.30
  179.2 1.7 collective-permute-done.32
  181.2 1.4 collective-permute-start.39
  182.6 1.7 collective-permute-start.36
  184.4 0.6 collective-permute-start.37
  185.0 9.1 %collective-permute-done.28 = bf16[2,512,256]{2,1,0:T(8,128)(2,1)S(1)} collective-permute-done((bf16[2,512,256]{2,1,0:T(8,128)(2,1)S(1)}, bf16[2,512,256]{2,1,0:T(8,128)(2,1)S(1)}, u32[]{:S(2)}, u32[]{:S(2)}) %collective-permute-start.28) | collective-permute-done | bytes 524320 | tf_op jit(solution)/shard_map/ppermute | solution.py:50
  194.4 2.5 %collective-permute-start.38 = (bf16[512,256]{1,0:T(8,128)(2,1)S(1)}, bf16[512,256]{1,0:T(8,128)(2,1)S(1)}, u32[]{:S(2)}, u32[]{:S(2)}) collective-permute-start(bf16[512,256]{1,0:T(8,128)(2,1)S(1)} %slice_bitcast_fusion.4), channel_id=1, source_target_pairs={{0,32},{1,97},{2,34},{3,99},{4,36},{5,101},{6,38},{7,103},{8,40},{... | collective-permute-start | bytes 786440 | tf_op jit(solution)/shard_map/ppermute | solution.py:50
  197.2 2.1 collective-permute-start.35
  199.3 0.6 slice_add_fusion
  199.9 0.9 collective-permute-done.38
  201.0 0.8 copy.11
  201.8 4.4 %collective-permute-done.33 = bf16[512,256]{1,0:T(8,128)(2,1)S(1)} collective-permute-done((bf16[512,256]{1,0:T(8,128)(2,1)S(1)}, bf16[512,256]{1,0:T(8,128)(2,1)S(1)}, u32[]{:S(2)}, u32[]{:S(2)}) %collective-permute-start.33) | collective-permute-done | bytes 262176 | tf_op jit(solution)/shard_map/ppermute | solution.py:50
  206.2 2.2 %collective-permute-done.35 = bf16[512,256]{1,0:T(8,128)(2,1)S(1)} collective-permute-done((bf16[512,256]{1,0:T(8,128)(2,1)S(1)}, bf16[512,256]{1,0:T(8,128)(2,1)S(1)}, u32[]{:S(2)}, u32[]{:S(2)}) %collective-permute-start.35) | collective-permute-done | bytes 262176 | tf_op jit(solution)/shard_map/ppermute | solution.py:50
  208.6 0.8 copy.10
  (98 shorter events, 4.4 us)
Async XLA Ops:
  7.2 61.2 %copy-start.9 = (bf16[31,512]{1,0:T(8,128)(2,1)S(1)}, bf16[31,512]{1,0:T(8,128)(2,1)}, u32[]{:S(2)}) copy-start(bf16[31,512]{1,0:T(8,128)(2,1)} %param.8) | copy-start | bytes 95236
  7.2 53.4 %all-gather.2.cloned.1.call-start = ((), (), s32[]{:S(2)}) async-start(), calls=%async_computation.1 | async-start | bytes 9437184 | tf_op jit(solution)/shard_map/all_gather | solution.py:336
  7.9 201.5 %reduce-scatter.2.cloned.1.call-start = ((), (), s32[]{:S(2)}) async-start(), calls=%async_computation.2 | async-start | bytes 9437184 | tf_op jit(solution)/shard_map/reduce_scatter | solution.py:362
  8.0 8.3 %collective-permute-start = (bf16[256,512]{1,0:T(8,128)(2,1)}, bf16[256,512]{1,0:T(8,128)(2,1)S(1)}, u32[]{:S(2)}, u32[]{:S(2)}) collective-permute-start(bf16[256,512]{1,0:T(8,128)(2,1)} %param.6), channel_id=1, source_target_pairs={{0,8},{1,9},{2,10},{3,11},{4,12},{5,13},{6,14},{7,15},{8,16},{9,17... | collective-permute-start | bytes 786440 | tf_op jit(solution)/shard_map/ppermute | solution.py:50
  9.6 8.3 %collective-permute-start.1 = (bf16[256,512]{1,0:T(8,128)(2,1)}, bf16[256,512]{1,0:T(8,128)(2,1)S(1)}, u32[]{:S(2)}, u32[]{:S(2)}) collective-permute-start(bf16[256,512]{1,0:T(8,128)(2,1)} %param.6), channel_id=1, source_target_pairs={{0,24},{1,25},{2,26},{3,27},{4,28},{5,29},{6,30},{7,31},{8,0},{9,1... | collective-permute-start | bytes 786440 | tf_op jit(solution)/shard_map/ppermute | solution.py:50
  10.1 8.4 %collective-permute-start.4 = (bf16[256,512]{1,0:T(8,128)(2,1)}, bf16[256,512]{1,0:T(8,128)(2,1)S(1)}, u32[]{:S(2)}, u32[]{:S(2)}) collective-permute-start(bf16[256,512]{1,0:T(8,128)(2,1)} %param.7), channel_id=1, source_target_pairs={{0,32},{1,33},{2,34},{3,35},{4,36},{5,37},{6,38},{7,39},{8,40},{9,... | collective-permute-start | bytes 786440 | tf_op jit(solution)/shard_map/ppermute | solution.py:50
  12.0 8.5 %collective-permute-start.5 = (bf16[256,512]{1,0:T(8,128)(2,1)}, bf16[256,512]{1,0:T(8,128)(2,1)S(1)}, u32[]{:S(2)}, u32[]{:S(2)}) collective-permute-start(bf16[256,512]{1,0:T(8,128)(2,1)} %param.7), channel_id=1, source_target_pairs={{0,96},{1,97},{2,98},{3,99},{4,100},{5,101},{6,102},{7,103},{8,104... | collective-permute-start | bytes 786440 | tf_op jit(solution)/shard_map/ppermute | solution.py:50
  16.3 5.0 %collective-permute-start.2 = (bf16[128,512]{1,0:T(8,128)(2,1)S(1)}, bf16[128,512]{1,0:T(8,128)(2,1)S(1)}, u32[]{:S(2)}, u32[]{:S(2)}) collective-permute-start(bf16[128,512]{1,0:T(8,128)(2,1)S(1)} %slice.148), channel_id=1, source_target_pairs={{0,8},{1,9},{2,10},{3,11},{4,12},{5,13},{6,14},{7,15},{8,16},{9,17... | collective-permute-start | bytes 393224 | tf_op jit(solution)/shard_map/ppermute | solution.py:50
  18.0 5.0 %collective-permute-start.3 = (bf16[128,512]{1,0:T(8,128)(2,1)S(1)}, bf16[128,512]{1,0:T(8,128)(2,1)S(1)}, u32[]{:S(2)}, u32[]{:S(2)}) collective-permute-start(bf16[128,512]{1,0:T(8,128)(2,1)S(1)} %slice.149), channel_id=1, source_target_pairs={{0,24},{1,25},{2,26},{3,27},{4,28},{5,29},{6,30},{7,31},{8,0},{9,1... | collective-permute-start | bytes 393224 | tf_op jit(solution)/shard_map/ppermute | solution.py:50
  18.5 5.0 %collective-permute-start.6 = (bf16[128,512]{1,0:T(8,128)(2,1)S(1)}, bf16[128,512]{1,0:T(8,128)(2,1)S(1)}, u32[]{:S(2)}, u32[]{:S(2)}) collective-permute-start(bf16[128,512]{1,0:T(8,128)(2,1)S(1)} %slice.150), channel_id=1, source_target_pairs={{0,32},{1,33},{2,34},{3,35},{4,36},{5,37},{6,38},{7,39},{8,40},{9,... | collective-permute-start | bytes 393224 | tf_op jit(solution)/shard_map/ppermute | solution.py:50
  20.5 5.0 %collective-permute-start.7 = (bf16[128,512]{1,0:T(8,128)(2,1)S(1)}, bf16[128,512]{1,0:T(8,128)(2,1)S(1)}, u32[]{:S(2)}, u32[]{:S(2)}) collective-permute-start(bf16[128,512]{1,0:T(8,128)(2,1)S(1)} %slice.151), channel_id=1, source_target_pairs={{0,96},{1,97},{2,98},{3,99},{4,100},{5,101},{6,102},{7,103},{8,104... | collective-permute-start | bytes 393224 | tf_op jit(solution)/shard_map/ppermute | solution.py:50
  26.6 28.8 %copy-start.7 = (bf16[1024,512]{1,0:T(8,128)(2,1)}, bf16[1024,512]{1,0:T(8,128)(2,1)S(1)}, u32[]{:S(2)}) copy-start(bf16[1024,512]{1,0:T(8,128)(2,1)S(1)} %constant_dynamic-update-slice_fusion.5) | copy-start | bytes 3145732
  26.6 23.8 %collective-permute-start.12 = (bf16[4,256,512]{2,1,0:T(8,128)(2,1)S(1)}, bf16[4,256,512]{2,1,0:T(8,128)(2,1)S(1)}, u32[]{:S(2)}, u32[]{:S(2)}) collective-permute-start(bf16[4,256,512]{2,1,0:T(8,128)(2,1)S(1)} %bitcast.96), channel_id=1, source_target_pairs={{0,8},{1,9},{2,10},{3,11},{4,12},{5,13},{6,14},{7,15},{8,16},{9,17... | collective-permute-start | bytes 3145736 | tf_op jit(solution)/shard_map/ppermute | solution.py:50
  28.3 22.8 %collective-permute-start.13 = (bf16[4,256,512]{2,1,0:T(8,128)(2,1)S(1)}, bf16[4,256,512]{2,1,0:T(8,128)(2,1)S(1)}, u32[]{:S(2)}, u32[]{:S(2)}) collective-permute-start(bf16[4,256,512]{2,1,0:T(8,128)(2,1)S(1)} %bitcast.97), channel_id=1, source_target_pairs={{0,24},{1,25},{2,26},{3,27},{4,28},{5,29},{6,30},{7,31},{8,0},{9,1... | collective-permute-start | bytes 3145736 | tf_op jit(solution)/shard_map/ppermute | solution.py:50
  30.8 24.6 %copy-start.8 = (bf16[1024,512]{1,0:T(8,128)(2,1)}, bf16[1024,512]{1,0:T(8,128)(2,1)S(1)}, u32[]{:S(2)}) copy-start(bf16[1024,512]{1,0:T(8,128)(2,1)S(1)} %constant_dynamic-update-slice_fusion) | copy-start | bytes 3145732
  30.8 22.8 %collective-permute-start.8 = (bf16[4,256,512]{2,1,0:T(8,128)(2,1)S(1)}, bf16[4,256,512]{2,1,0:T(8,128)(2,1)S(1)}, u32[]{:S(2)}, u32[]{:S(2)}) collective-permute-start(bf16[4,256,512]{2,1,0:T(8,128)(2,1)S(1)} %bitcast.99), channel_id=1, source_target_pairs={{0,32},{1,33},{2,34},{3,35},{4,36},{5,37},{6,38},{7,39},{8,40},{9,... | collective-permute-start | bytes 3145736 | tf_op jit(solution)/shard_map/ppermute | solution.py:50
  32.5 22.9 %collective-permute-start.9 = (bf16[4,256,512]{2,1,0:T(8,128)(2,1)S(1)}, bf16[4,256,512]{2,1,0:T(8,128)(2,1)S(1)}, u32[]{:S(2)}, u32[]{:S(2)}) collective-permute-start(bf16[4,256,512]{2,1,0:T(8,128)(2,1)S(1)} %bitcast.100), channel_id=1, source_target_pairs={{0,96},{1,97},{2,98},{3,99},{4,100},{5,101},{6,102},{7,103},{8,104... | collective-permute-start | bytes 3145736 | tf_op jit(solution)/shard_map/ppermute | solution.py:50
  50.4 5.0 %copy-start.2 = (bf16[4,256,512]{2,1,0:T(8,128)(2,1)}, bf16[4,256,512]{2,1,0:T(8,128)(2,1)S(1)}, u32[]{:S(2)}) copy-start(bf16[4,256,512]{2,1,0:T(8,128)(2,1)S(1)} %collective-permute-done.12.refs_6_) | copy-start | bytes 3145732
  50.4 14.7 %collective-permute-start.14 = (bf16[2,256,512]{2,1,0:T(8,128)(2,1)S(1)}, bf16[2,256,512]{2,1,0:T(8,128)(2,1)S(1)}, u32[]{:S(2)}, u32[]{:S(2)}) collective-permute-start(bf16[2,256,512]{2,1,0:T(8,128)(2,1)S(1)} %slice.154), channel_id=1, source_target_pairs={{0,8},{1,9},{2,10},{3,11},{4,12},{5,13},{6,14},{7,15},{8,16},{9,17... | collective-permute-start | bytes 1572872 | tf_op jit(solution)/shard_map/ppermute | solution.py:50
  51.1 2.5 %copy-start.3 = (bf16[4,256,512]{2,1,0:T(8,128)(2,1)}, bf16[4,256,512]{2,1,0:T(8,128)(2,1)S(1)}, u32[]{:S(2)}) copy-start(bf16[4,256,512]{2,1,0:T(8,128)(2,1)S(1)} %collective-permute-done.13.refs_7_) | copy-start | bytes 3145732
  51.1 17.9 %collective-permute-start.15 = (bf16[2,256,512]{2,1,0:T(8,128)(2,1)S(1)}, bf16[2,256,512]{2,1,0:T(8,128)(2,1)}, u32[]{:S(2)}, u32[]{:S(2)}) collective-permute-start(bf16[2,256,512]{2,1,0:T(8,128)(2,1)S(1)} %slice.155), channel_id=1, source_target_pairs={{0,24},{1,25},{2,26},{3,27},{4,28},{5,29},{6,30},{7,31},{8,0},{9,1... | collective-permute-start | bytes 1572872 | tf_op jit(solution)/shard_map/ppermute | solution.py:50
  53.6 1.8 copy-start.4
  53.6 15.4 %collective-permute-start.10 = (bf16[2,256,512]{2,1,0:T(8,128)(2,1)S(1)}, bf16[2,256,512]{2,1,0:T(8,128)(2,1)}, u32[]{:S(2)}, u32[]{:S(2)}) collective-permute-start(bf16[2,256,512]{2,1,0:T(8,128)(2,1)S(1)} %slice.152), channel_id=1, source_target_pairs={{0,32},{1,33},{2,34},{3,35},{4,36},{5,37},{6,38},{7,39},{8,40},{9,... | collective-permute-start | bytes 1572872 | tf_op jit(solution)/shard_map/ppermute | solution.py:50
  55.3 1.0 copy-start.5
  56.3 12.7 %collective-permute-start.11 = (bf16[2,256,512]{2,1,0:T(8,128)(2,1)S(1)}, bf16[2,256,512]{2,1,0:T(8,128)(2,1)}, u32[]{:S(2)}, u32[]{:S(2)}) collective-permute-start(bf16[2,256,512]{2,1,0:T(8,128)(2,1)S(1)} %slice.153), channel_id=1, source_target_pairs={{0,96},{1,97},{2,98},{3,99},{4,100},{5,101},{6,102},{7,103},{8,104... | collective-permute-start | bytes 1572872 | tf_op jit(solution)/shard_map/ppermute | solution.py:50
  61.6 11.2 %collective-permute-start.16 = (bf16[32,4608]{1,0:T(8,128)(2,1)S(1)}, bf16[32,4608]{1,0:T(8,128)(2,1)}, u32[]{:S(2)}, u32[]{:S(2)}) collective-permute-start(bf16[32,4608]{1,0:T(8,128)(2,1)S(1)} %pad_maximum_fusion), channel_id=1, source_target_pairs={{0,8},{8,16},{16,24},{24,32},{32,40},{40,48},{48,56},{56,64},{64,7... | collective-permute-start | bytes 884744 | tf_op jit(solution)/shard_map/ppermute | solution.py:59
  65.1 10.8 %copy-start.10 = (bf16[2,256,512]{2,1,0:T(8,128)(2,1)}, bf16[2,256,512]{2,1,0:T(8,128)(2,1)S(1)}, u32[]{:S(2)}) copy-start(bf16[2,256,512]{2,1,0:T(8,128)(2,1)S(1)} %collective-permute-done.14.refs_8_) | copy-start | bytes 1572868
  65.1 10.8 %collective-permute-start.17 = (bf16[32,4608]{1,0:T(8,128)(2,1)S(1)}, bf16[32,4608]{1,0:T(8,128)(2,1)S(1)}, u32[]{:S(2)}, u32[]{:S(2)}) collective-permute-start(bf16[32,4608]{1,0:T(8,128)(2,1)S(1)} %pad_maximum_fusion.1), channel_id=1, source_target_pairs={{8,0},{16,8},{24,16},{32,24},{40,32},{48,40},{56,48},{64,56},{72,6... | collective-permute-start | bytes 884744 | tf_op jit(solution)/shard_map/ppermute | solution.py:59
  75.9 0.7 copy-start.11
  131.9 1.3 copy-start.6
  131.9 2.0 copy-start.1
  133.3 20.9 %collective-permute-start.18 = (f32[32,512]{1,0:T(8,128)S(1)}, f32[32,512]{1,0:T(8,128)S(1)}, u32[]{:S(2)}, u32[]{:S(2)}) collective-permute-start(f32[32,512]{1,0:T(8,128)S(1)} %copy-done.6), channel_id=1, source_target_pairs={{0,8},{8,0},{16,24},{24,16},{32,40},{40,32},{48,56},{56,48},{64,72... | collective-permute-start | bytes 196616 | tf_op jit(solution)/shard_map/ppermute | solution.py:366
  135.1 19.2 %collective-permute-start.21 = (bf16[2,512,256]{2,1,0:T(8,128)(2,1)}, bf16[2,512,256]{2,1,0:T(8,128)(2,1)S(1)}, u32[]{:S(2)}, u32[]{:S(2)}) collective-permute-start(bf16[2,512,256]{2,1,0:T(8,128)(2,1)} %get-tuple-element.101), channel_id=1, source_target_pairs={{0,32},{1,97},{2,34},{3,99},{4,36},{5,101},{6,38},{7,103},{8,40},{... | collective-permute-start | bytes 1572872 | tf_op jit(solution)/shard_map/ppermute | solution.py:50
  136.6 17.6 %collective-permute-start.22 = (bf16[2,512,256]{2,1,0:T(8,128)(2,1)}, bf16[2,512,256]{2,1,0:T(8,128)(2,1)S(1)}, u32[]{:S(2)}, u32[]{:S(2)}) collective-permute-start(bf16[2,512,256]{2,1,0:T(8,128)(2,1)} %get-tuple-element.100), channel_id=1, source_target_pairs={{0,8},{1,25},{2,10},{3,27},{4,12},{5,29},{6,14},{7,31},{8,16},{9,1... | collective-permute-start | bytes 1572872 | tf_op jit(solution)/shard_map/ppermute | solution.py:50
  140.4 17.8 %collective-permute-start.19 = (bf16[2,512,256]{2,1,0:T(8,128)(2,1)S(1)}, bf16[2,512,256]{2,1,0:T(8,128)(2,1)S(1)}, u32[]{:S(2)}, u32[]{:S(2)}) collective-permute-start(bf16[2,512,256]{2,1,0:T(8,128)(2,1)S(1)} %get-tuple-element.103), channel_id=1, source_target_pairs={{0,32},{1,97},{2,34},{3,99},{4,36},{5,101},{6,38},{7,103},{8,40},{... | collective-permute-start | bytes 1572872 | tf_op jit(solution)/shard_map/ppermute | solution.py:50
  140.4 17.8 %collective-permute-start.20 = (bf16[2,512,256]{2,1,0:T(8,128)(2,1)S(1)}, bf16[2,512,256]{2,1,0:T(8,128)(2,1)S(1)}, u32[]{:S(2)}, u32[]{:S(2)}) collective-permute-start(bf16[2,512,256]{2,1,0:T(8,128)(2,1)S(1)} %get-tuple-element.102), channel_id=1, source_target_pairs={{0,8},{1,25},{2,10},{3,27},{4,12},{5,29},{6,14},{7,31},{8,16},{9,1... | collective-permute-start | bytes 1572872 | tf_op jit(solution)/shard_map/ppermute | solution.py:50
  154.2 14.1 %copy-start = (bf16[6,4,512,256]{3,2,1,0:T(8,128)(2,1)S(1)}, bf16[6,4,512,256]{3,2,1,0:T(8,128)(2,1)}, u32[]{:S(2)}) copy-start(bf16[6,4,512,256]{3,2,1,0:T(8,128)(2,1)} %shard_map.93) | copy-start | bytes 18874372
  155.8 12.4 %collective-permute-start.26 = (bf16[2,512,256]{2,1,0:T(8,128)(2,1)S(1)}, bf16[2,512,256]{2,1,0:T(8,128)(2,1)S(1)}, u32[]{:S(2)}, u32[]{:S(2)}) collective-permute-start(bf16[2,512,256]{2,1,0:T(8,128)(2,1)S(1)} %get-tuple-element.99), channel_id=1, source_target_pairs={{0,32},{1,97},{2,34},{3,99},{4,36},{5,101},{6,38},{7,103},{8,40},{... | collective-permute-start | bytes 1572872 | tf_op jit(solution)/shard_map/ppermute | solution.py:50
  158.1 10.1 %collective-permute-start.27 = (bf16[2,512,256]{2,1,0:T(8,128)(2,1)S(1)}, bf16[2,512,256]{2,1,0:T(8,128)(2,1)S(1)}, u32[]{:S(2)}, u32[]{:S(2)}) collective-permute-start(bf16[2,512,256]{2,1,0:T(8,128)(2,1)S(1)} %get-tuple-element.98), channel_id=1, source_target_pairs={{0,8},{1,25},{2,10},{3,27},{4,12},{5,29},{6,14},{7,31},{8,16},{9,1... | collective-permute-start | bytes 1572872 | tf_op jit(solution)/shard_map/ppermute | solution.py:50
  159.7 12.9 %collective-permute-start.23 = (bf16[2,512,256]{2,1,0:T(8,128)(2,1)S(1)}, bf16[2,512,256]{2,1,0:T(8,128)(2,1)S(1)}, u32[]{:S(2)}, u32[]{:S(2)}) collective-permute-start(bf16[2,512,256]{2,1,0:T(8,128)(2,1)S(1)} %get-tuple-element.97), channel_id=1, source_target_pairs={{0,32},{1,97},{2,34},{3,99},{4,36},{5,101},{6,38},{7,103},{8,40},{... | collective-permute-start | bytes 1572872 | tf_op jit(solution)/shard_map/ppermute | solution.py:50
  161.6 6.6 %collective-permute-start.25 = (f32[32,512]{1,0:T(8,128)S(1)}, f32[32,512]{1,0:T(8,128)S(1)}, u32[]{:S(2)}, u32[]{:S(2)}) collective-permute-start(f32[32,512]{1,0:T(8,128)S(1)} %add.221), channel_id=1, source_target_pairs={{0,16},{8,24},{16,0},{24,8},{32,48},{40,56},{48,32},{56,40},{64,80... | collective-permute-start | bytes 196616 | tf_op jit(solution)/shard_map/ppermute | solution.py:366
  165.2 9.2 %collective-permute-start.24 = (bf16[2,512,256]{2,1,0:T(8,128)(2,1)S(1)}, bf16[2,512,256]{2,1,0:T(8,128)(2,1)S(1)}, u32[]{:S(2)}, u32[]{:S(2)}) collective-permute-start(bf16[2,512,256]{2,1,0:T(8,128)(2,1)S(1)} %get-tuple-element.96), channel_id=1, source_target_pairs={{0,8},{1,25},{2,10},{3,27},{4,12},{5,29},{6,14},{7,31},{8,16},{9,1... | collective-permute-start | bytes 1572872 | tf_op jit(solution)/shard_map/ppermute | solution.py:50
  168.5 10.7 %collective-permute-start.31 = (bf16[2,512,256]{2,1,0:T(8,128)(2,1)S(1)}, bf16[2,512,256]{2,1,0:T(8,128)(2,1)S(1)}, u32[]{:S(2)}, u32[]{:S(2)}) collective-permute-start(bf16[2,512,256]{2,1,0:T(8,128)(2,1)S(1)} %get-tuple-element.95), channel_id=1, source_target_pairs={{0,32},{1,97},{2,34},{3,99},{4,36},{5,101},{6,38},{7,103},{8,40},{... | collective-permute-start | bytes 1572872 | tf_op jit(solution)/shard_map/ppermute | solution.py:50
  170.3 10.6 %collective-permute-start.32 = (bf16[2,512,256]{2,1,0:T(8,128)(2,1)S(1)}, bf16[2,512,256]{2,1,0:T(8,128)(2,1)S(1)}, u32[]{:S(2)}, u32[]{:S(2)}) collective-permute-start(bf16[2,512,256]{2,1,0:T(8,128)(2,1)S(1)} %get-tuple-element.94), channel_id=1, source_target_pairs={{0,8},{1,25},{2,10},{3,27},{4,12},{5,29},{6,14},{7,31},{8,16},{9,1... | collective-permute-start | bytes 1572872 | tf_op jit(solution)/shard_map/ppermute | solution.py:50
  174.7 4.5 %collective-permute-start.30 = (f32[32,512]{1,0:T(8,128)S(1)}, f32[32,512]{1,0:T(8,128)S(1)}, u32[]{:S(2)}, u32[]{:S(2)}) collective-permute-start(f32[32,512]{1,0:T(8,128)S(1)} %add.226), channel_id=1, source_target_pairs={{0,32},{8,40},{16,48},{24,56},{32,0},{40,8},{48,16},{56,24},{64,96... | collective-permute-start | bytes 196616 | tf_op jit(solution)/shard_map/ppermute | solution.py:366
  175.3 18.8 %collective-permute-start.28 = (bf16[2,512,256]{2,1,0:T(8,128)(2,1)S(1)}, bf16[2,512,256]{2,1,0:T(8,128)(2,1)S(1)}, u32[]{:S(2)}, u32[]{:S(2)}) collective-permute-start(bf16[2,512,256]{2,1,0:T(8,128)(2,1)S(1)} %get-tuple-element.93), channel_id=1, source_target_pairs={{0,32},{1,97},{2,34},{3,99},{4,36},{5,101},{6,38},{7,103},{8,40},{... | collective-permute-start | bytes 1572872 | tf_op jit(solution)/shard_map/ppermute | solution.py:50
  177.5 16.6 %collective-permute-start.29 = (bf16[2,512,256]{2,1,0:T(8,128)(2,1)S(1)}, bf16[2,512,256]{2,1,0:T(8,128)(2,1)S(1)}, u32[]{:S(2)}, u32[]{:S(2)}) collective-permute-start(bf16[2,512,256]{2,1,0:T(8,128)(2,1)S(1)} %get-tuple-element.92), channel_id=1, source_target_pairs={{0,8},{1,25},{2,10},{3,27},{4,12},{5,29},{6,14},{7,31},{8,16},{9,1... | collective-permute-start | bytes 1572872 | tf_op jit(solution)/shard_map/ppermute | solution.py:50
  181.2 15.9 %collective-permute-start.39 = (f32[32,512]{1,0:T(8,128)S(1)}, f32[32,512]{1,0:T(8,128)S(1)}, u32[]{:S(2)}, u32[]{:S(2)}) collective-permute-start(f32[32,512]{1,0:T(8,128)S(1)} %add.231), channel_id=1, source_target_pairs={{0,64},{8,72},{16,80},{24,88},{32,96},{40,104},{48,112},{56,120},{... | collective-permute-start | bytes 196616 | tf_op jit(solution)/shard_map/ppermute | solution.py:366
  182.6 14.6 %collective-permute-start.36 = (bf16[512,256]{1,0:T(8,128)(2,1)S(1)}, bf16[512,256]{1,0:T(8,128)(2,1)S(1)}, u32[]{:S(2)}, u32[]{:S(2)}) collective-permute-start(bf16[512,256]{1,0:T(8,128)(2,1)S(1)} %get-tuple-element.106), channel_id=1, source_target_pairs={{0,96},{1,33},{2,98},{3,35},{4,100},{5,37},{6,102},{7,39},{8,104},... | collective-permute-start | bytes 786440 | tf_op jit(solution)/shard_map/ppermute | solution.py:50
  184.4 15.5 %collective-permute-start.37 = (bf16[512,256]{1,0:T(8,128)(2,1)S(1)}, bf16[512,256]{1,0:T(8,128)(2,1)S(1)}, u32[]{:S(2)}, u32[]{:S(2)}) collective-permute-start(bf16[512,256]{1,0:T(8,128)(2,1)S(1)} %get-tuple-element.107), channel_id=1, source_target_pairs={{0,64},{1,65},{2,66},{3,67},{4,68},{5,69},{6,70},{7,71},{8,72},{9,... | collective-permute-start | bytes 786440 | tf_op jit(solution)/shard_map/ppermute | solution.py:50
  194.4 6.4 %collective-permute-start.38 = (bf16[512,256]{1,0:T(8,128)(2,1)S(1)}, bf16[512,256]{1,0:T(8,128)(2,1)S(1)}, u32[]{:S(2)}, u32[]{:S(2)}) collective-permute-start(bf16[512,256]{1,0:T(8,128)(2,1)S(1)} %slice_bitcast_fusion.4), channel_id=1, source_target_pairs={{0,32},{1,97},{2,34},{3,99},{4,36},{5,101},{6,38},{7,103},{8,40},{... | collective-permute-start | bytes 786440 | tf_op jit(solution)/shard_map/ppermute | solution.py:50
  197.0 9.2 %collective-permute-start.33 = (bf16[512,256]{1,0:T(8,128)(2,1)S(1)}, bf16[512,256]{1,0:T(8,128)(2,1)S(1)}, u32[]{:S(2)}, u32[]{:S(2)}) collective-permute-start(bf16[512,256]{1,0:T(8,128)(2,1)S(1)} %get-tuple-element.108), channel_id=1, source_target_pairs={{0,24},{1,9},{2,26},{3,11},{4,28},{5,13},{6,30},{7,15},{8,0},{9,17... | collective-permute-start | bytes 786440 | tf_op jit(solution)/shard_map/ppermute | solution.py:50
  197.1 9.1 %collective-permute-start.34 = (bf16[512,256]{1,0:T(8,128)(2,1)S(1)}, bf16[512,256]{1,0:T(8,128)(2,1)S(1)}, u32[]{:S(2)}, u32[]{:S(2)}) collective-permute-start(bf16[512,256]{1,0:T(8,128)(2,1)S(1)} %get-tuple-element.109), channel_id=1, source_target_pairs={{0,16},{1,17},{2,18},{3,19},{4,20},{5,21},{6,22},{7,23},{8,24},{9,... | collective-permute-start | bytes 786440 | tf_op jit(solution)/shard_map/ppermute | solution.py:50
  197.2 11.3 %collective-permute-start.35 = (bf16[512,256]{1,0:T(8,128)(2,1)S(1)}, bf16[512,256]{1,0:T(8,128)(2,1)S(1)}, u32[]{:S(2)}, u32[]{:S(2)}) collective-permute-start(bf16[512,256]{1,0:T(8,128)(2,1)S(1)} %slice_bitcast_fusion.6), channel_id=1, source_target_pairs={{0,8},{1,25},{2,10},{3,27},{4,12},{5,29},{6,14},{7,31},{8,16},{9,1... | collective-permute-start | bytes 786440 | tf_op jit(solution)/shard_map/ppermute | solution.py:50
Sparse Core Ops, SparseCore 0:
  9.7 50.7 all-gather.1
  132.1 52.7 reduce-scatter.1
